TPU v7x, 32 devices: a whole 2x2x4 slice. The times are simulated.
32 devices in a mesh: section: 2 (over core), dp: 16 (over z, y, x).
Axes of the slice: x: 2, y: 2, z: 4, core: 2. Of those that a mesh axis runs over, the one named last changes fastest.
Arguments:
- frames: bfloat16 [16, 1024, 80], P('dp'), may hold values from -6 to 6
- targets: int32 [16, 1024], P('dp'), may hold values from 0 to 1023
- lengths: int32 [16], P('dp'), may hold values from 128 to 1024, as said below
- w_attn: float32 [2, 512, 1536], P('section', 'dp'), may hold values from -0.25 to 0.25
- w_out: float32 [2, 512, 512], P('section', 'dp'), may hold values from -0.75 to 0.75
- w_pos: float32 [2, 512, 512], P('section', 'dp'), may hold values from -0.25 to 0.25
- w_up: float32 [2, 512, 2048], P('section', 'dp'), may hold values from -0.25 to 0.25
- w_down: float32 [2, 2048, 512], P('section', 'dp'), may hold values from -0.125 to 0.125
- layer_vecs: float32 [2, 4, 512], P('section', None, 'dp'), may hold values from -1.5 to 3.125
- w_in: float32 [80, 512], P(None, 'dp'), may hold values from -0.625 to 0.625
- w_head: float32 [512, 1024], P('dp'), may hold values from -0.25 to 0.25
- gain_final: float32 [512], P('dp'), may hold values from 0.4 to 3.125
- moment_attn: float32 [2, 512, 1536], P('section', 'dp'), may hold values from -4.7683716e-06 to 4.7683716e-06
- moment_out: float32 [2, 512, 512], P('section', 'dp'), may hold values from -4.7683716e-06 to 4.7683716e-06
- moment_pos: float32 [2, 512, 512], P('section', 'dp'), may hold values from -4.7683716e-06 to 4.7683716e-06
- moment_up: float32 [2, 512, 2048], P('section', 'dp'), may hold values from -4.7683716e-06 to 4.7683716e-06
- moment_down: float32 [2, 2048, 512], P('section', 'dp'), may hold values from -4.7683716e-06 to 4.7683716e-06
- moment_vecs: float32 [2, 4, 512], P('section', None, 'dp'), may hold values from -1.9073486e-05 to 1.9073486e-05
- moment_in: float32 [80, 512], P(None, 'dp'), may hold values from -4.7683716e-06 to 4.7683716e-06
- moment_head: float32 [512, 1024], P('dp'), may hold values from -4.7683716e-06 to 4.7683716e-06
- moment_final: float32 [512], P('dp'), may hold values from -1.9073486e-05 to 1.9073486e-05
- second_attn: float32 [2, 512, 1536], P('section', 'dp'), may hold values from 5.4159446e-14 to 2.1663778e-13
- second_out: float32 [2, 512, 512], P('section', 'dp'), may hold values from 5.4159446e-14 to 2.1663778e-13
- second_pos: float32 [2, 512, 512], P('section', 'dp'), may hold values from 2.7079722e-15 to 1.0831889e-14
- second_up: float32 [2, 512, 2048], P('section', 'dp'), may hold values from 5.4159446e-14 to 2.1663778e-13
- second_down: float32 [2, 2048, 512], P('section', 'dp'), may hold values from 5.4159446e-14 to 2.1663778e-13
- second_vecs: float32 [2, 4, 512], P('section', None, 'dp'), may hold values from 8.6655113e-13 to 3.4662045e-12
- second_in: float32 [80, 512], P(None, 'dp'), may hold values from 5.4159446e-14 to 2.1663778e-13
- second_head: float32 [512, 1024], P('dp'), may hold values from 5.4159446e-14 to 2.1663778e-13
- second_final: float32 [512], P('dp'), may hold values from 8.6655113e-13 to 3.4662045e-12
Outputs:
- new_attn: float32 [2, 512, 1536], P('section', 'dp')
- new_out: float32 [2, 512, 512], P('section', 'dp')
- new_pos: float32 [2, 512, 512], P('section', 'dp')
- new_up: float32 [2, 512, 2048], P('section', 'dp')
- new_down: float32 [2, 2048, 512], P('section', 'dp')
- new_vecs: float32 [2, 4, 512], P('section', None, 'dp')
- new_in: float32 [80, 512], P(None, 'dp')
- new_head: float32 [512, 1024], P('dp')
- new_final: float32 [512], P('dp')
- new_moment_attn: float32 [2, 512, 1536], P('section', 'dp')
- new_moment_out: float32 [2, 512, 512], P('section', 'dp')
- new_moment_pos: float32 [2, 512, 512], P('section', 'dp')
- new_moment_up: float32 [2, 512, 2048], P('section', 'dp')
- new_moment_down: float32 [2, 2048, 512], P('section', 'dp')
- new_moment_vecs: float32 [2, 4, 512], P('section', None, 'dp')
- new_moment_in: float32 [80, 512], P(None, 'dp')
- new_moment_head: float32 [512, 1024], P('dp')
- new_moment_final: float32 [512], P('dp')
- new_second_attn: float32 [2, 512, 1536], P('section', 'dp')
- new_second_out: float32 [2, 512, 512], P('section', 'dp')
- new_second_pos: float32 [2, 512, 512], P('section', 'dp')
- new_second_up: float32 [2, 512, 2048], P('section', 'dp')
- new_second_down: float32 [2, 2048, 512], P('section', 'dp')
- new_second_vecs: float32 [2, 4, 512], P('section', None, 'dp')
- new_second_in: float32 [80, 512], P(None, 'dp')
- new_second_head: float32 [512, 1024], P('dp')
- new_second_final: float32 [512], P('dp')
- grad_norm: float32 [], replicated
- loss_sum: float32 [], replicated
Inputs may be any that keep to these rules, and one draw needn't show every extreme that they name: `lengths`: one stream has exactly 1024 valid frames.
All inputs are finite; a program needn't handle non-finite values.
Results may differ from a plain program's by a relative error of at most 0.012.
The roundings to bfloat16 on the way count: a program that leaves them out, or rounds other values in their place, can miss the bound.
Values may be sent and summed in bfloat16 or wider, within the bound.
No kernel may reach another device: no remote copies, remote signals or barrier semaphores. Data moves between devices by JAX's collectives and lax.ppermute only.
A program may use at most 192 MiB of HBM per device.

v0:
```python
import jax
import jax.numpy as jnp
from jax import lax
from jax.sharding import PartitionSpec as P

D = 512
HEADS = 8
HEAD_DIM = 64
MEM = 256
SEG = 512
SEGS = 2
STEP = 10


NEG = -1e30
CLIP = 0.02


def from_behind(value, axis, steps):
    count = lax.axis_size(axis)
    initial, last = (max(0, -steps), min(count, count - steps))
    return lax.ppermute(value, axis, [(source, source + steps) for source in range(initial, last)])


def matmul(left, right):
    return jnp.dot(left, right, preferred_element_type=jnp.float32)


def tdot(left, right):
    return lax.dot_general(
        left, right, (((0,), (0,)), ((), ())), preferred_element_type=jnp.float32
    )


def dott(left, right):
    return lax.dot_general(
        left, right, (((1,), (1,)), ((), ())), preferred_element_type=jnp.float32
    )


def einmul(form, left, right):
    return jnp.einsum(form, left, right, preferred_element_type=jnp.float32)


def norm_gain(values, gain):
    center = values - jnp.mean(values, -1, keepdims=True)
    spread = jnp.mean(center * center, -1, keepdims=True)
    return center * lax.rsqrt(spread + 1e-05) * gain


def sinus_table():
    count = MEM + SEG
    where_at = (count - 1 - jnp.arange(count, dtype=jnp.int32)).astype(jnp.float32)[:, None]
    freqs = jnp.exp(
        -jnp.log(10000.0) * (2.0 * jnp.arange(D // 2, dtype=jnp.int32).astype(jnp.float32) / D)
    )
    angles = where_at * freqs[None, :]
    return jnp.concatenate([jnp.sin(angles), jnp.cos(angles)], 1)


def key_mask(segment, length):
    rows = jnp.arange(SEG, dtype=jnp.int32)[:, None]
    joint = jnp.arange(MEM + SEG, dtype=jnp.int32)[None, :]
    segment = jnp.asarray(segment, jnp.int32)
    spot = jnp.where(
        joint < MEM, (segment - 1) * SEG + SEG - MEM + joint, segment * SEG + joint - MEM
    )
    return (spot < length) & ((joint >= MEM) | (segment >= 1)) & (joint <= MEM + rows)


def row_weight(segment, length):
    spot = jnp.asarray(segment, jnp.int32) * SEG + jnp.arange(SEG, dtype=jnp.int32)
    return (spot < length).astype(jnp.float32) / length.astype(jnp.float32)


def skew(block):
    count, rows, cols = block.shape
    lead = rows - 1
    flat = jnp.pad(block, ((0, 0), (0, 0), (0, 1))).reshape(count, rows * (cols + 1))
    return flat[:, lead : lead + rows * cols].reshape(count, rows, cols)


def unskew(grad):
    count, rows, cols = grad.shape
    lead = rows - 1
    flat = jnp.pad(grad.reshape(count, rows * cols), ((0, 0), (lead, rows - lead)))
    return flat.reshape(count, rows, cols + 1)[:, :, :cols]


def slab(block, pair):
    width = 2 * HEAD_DIM
    return lax.dynamic_slice_in_dim(block, pair * width, width, 1).reshape(
        block.shape[0], 2, HEAD_DIM
    )


def put_slab(block, piece, pair):
    width = 2 * HEAD_DIM
    return lax.dynamic_update_slice_in_dim(
        block, piece.reshape(piece.shape[0], width), pair * width, 1
    )


def pair_scores(part_qu, part_qv, part_keys, part_rel, mask):
    content = einmul("ihd,jhd->hij", part_qu, part_keys)
    position = skew(einmul("ihd,jhd->hij", part_qv, part_rel))
    return jnp.where(mask[None], (content + position) * HEAD_DIM ** (-0.5), NEG)


def attend(query_u, query_v, keys, values, rel, mask):
    rows = query_u.shape[0]

    def one_pair(pair, carry):
        outputs, sums = carry
        scores = pair_scores(
            slab(query_u, pair), slab(query_v, pair), slab(keys, pair), slab(rel, pair), mask
        )
        top = jnp.max(scores, -1, keepdims=True)
        expo = jnp.exp(scores - top)
        total = jnp.sum(expo, -1, keepdims=True)
        probs = (expo / total).astype(jnp.bfloat16)
        piece = einmul("hij,jhd->ihd", probs, slab(values, pair))
        outputs = put_slab(outputs, piece, pair)
        sums = lax.dynamic_update_slice_in_dim(sums, (top + jnp.log(total))[:, :, 0], pair * 2, 0)
        return (outputs, sums)

    start = (jnp.zeros((rows, D), jnp.float32), jnp.zeros((HEADS, rows), jnp.float32))
    return lax.fori_loop(0, HEADS // 2, one_pair, start)


def attend_back(query_u, query_v, keys, values, rel, mask, sums, grad_att):
    rows = query_u.shape[0]
    cols = keys.shape[0]

    def one_pair(pair, carry):
        acc_qu, acc_qv, acc_keys, acc_values, acc_rel = carry
        part_qu = slab(query_u, pair)
        part_qv = slab(query_v, pair)
        part_keys = slab(keys, pair)
        part_values = slab(values, pair)
        part_rel = slab(rel, pair)
        scores = pair_scores(part_qu, part_qv, part_keys, part_rel, mask)
        probs = jnp.exp(scores - lax.dynamic_slice_in_dim(sums, pair * 2, 2, 0)[:, :, None])
        part_grad = slab(grad_att, pair)
        grad_values = einmul("hij,ihd->jhd", probs.astype(jnp.bfloat16), part_grad)
        grad_probs = einmul("ihd,jhd->hij", part_grad, part_values)
        inner_sum = jnp.sum(probs * grad_probs, -1, keepdims=True)
        grad_scores = jnp.where(mask[None], probs * (grad_probs - inner_sum), 0.0) * HEAD_DIM ** (
            -0.5
        )
        grad_content = grad_scores.astype(jnp.bfloat16)
        grad_position = unskew(grad_scores).astype(jnp.bfloat16)
        acc_qu = put_slab(acc_qu, einmul("hij,jhd->ihd", grad_content, part_keys), pair)
        acc_keys = put_slab(acc_keys, einmul("hij,ihd->jhd", grad_content, part_qu), pair)
        acc_qv = put_slab(acc_qv, einmul("hij,jhd->ihd", grad_position, part_rel), pair)
        acc_rel = put_slab(acc_rel, einmul("hij,ihd->jhd", grad_position, part_qv), pair)
        acc_values = put_slab(acc_values, grad_values, pair)
        return (acc_qu, acc_qv, acc_keys, acc_values, acc_rel)

    start = (
        jnp.zeros((rows, D), jnp.float32),
        jnp.zeros((rows, D), jnp.float32),
        jnp.zeros((cols, D), jnp.float32),
        jnp.zeros((cols, D), jnp.float32),
        jnp.zeros((cols, D), jnp.float32),
    )
    return lax.fori_loop(0, HEADS // 2, one_pair, start)


def layer_pass(hidden, memory, segment, length, weights):
    w_attn, w_out, w_pos, w_up, w_down, vectors = weights
    gains = vectors.astype(jnp.float32)
    joined = jnp.concatenate([memory, hidden], 0)
    normed, norm_one_back = jax.vjp(norm_gain, joined, gains[0])
    normed_b = normed.astype(jnp.bfloat16)
    query = matmul(normed_b[MEM:], w_attn[:, :D])
    key_val = matmul(normed_b, w_attn[:, D:])
    keys = key_val[:, :D].astype(jnp.bfloat16)
    values = key_val[:, D:].astype(jnp.bfloat16)
    query_u = (query + gains[2]).astype(jnp.bfloat16)
    query_v = (query + gains[3]).astype(jnp.bfloat16)
    table = sinus_table().astype(jnp.bfloat16)
    rel = matmul(table, w_pos).astype(jnp.bfloat16)
    mask = key_mask(segment, length)
    attended, sums = attend(query_u, query_v, keys, values, rel, mask)
    attended_b = attended.astype(jnp.bfloat16)
    mixed = hidden + matmul(attended_b, w_out)
    normed_two, norm_two_back = jax.vjp(norm_gain, mixed, gains[1])
    normed_two_b = normed_two.astype(jnp.bfloat16)
    inner = matmul(normed_two_b, w_up)
    activated, gelu_back = jax.vjp(jax.nn.gelu, inner)
    activated_b = activated.astype(jnp.bfloat16)
    output = mixed + matmul(activated_b, w_down)
    saved = (
        normed_b,
        query_u,
        query_v,
        keys,
        values,
        table,
        rel,
        mask,
        sums,
        attended_b,
        normed_two_b,
        activated_b,
        norm_one_back,
        norm_two_back,
        gelu_back,
    )
    return (output, saved)


def layer_back(saved, grad_out, weights):
    w_attn, w_out, w_pos, w_up, w_down, vectors = weights
    (
        normed_b,
        query_u,
        query_v,
        keys,
        values,
        table,
        rel,
        mask,
        sums,
        attended_b,
        normed_two_b,
        activated_b,
        norm_one_back,
        norm_two_back,
        gelu_back,
    ) = saved
    grad_y = grad_out.astype(jnp.bfloat16)
    grad_down = tdot(activated_b, grad_y)
    (grad_inner,) = gelu_back(dott(grad_y, w_down))
    grad_inner_b = grad_inner.astype(jnp.bfloat16)
    grad_up = tdot(normed_two_b, grad_inner_b)
    grad_mixed, grad_gain_two = norm_two_back(dott(grad_inner_b, w_up))
    grad_mixed = grad_mixed + grad_out
    grad_att = grad_mixed.astype(jnp.bfloat16)
    grad_wout = tdot(attended_b, grad_att)
    grad_attended = dott(grad_att, w_out).astype(jnp.bfloat16)
    grad_qu, grad_qv, grad_keys, grad_values, grad_rel = attend_back(
        query_u, query_v, keys, values, rel, mask, sums, grad_attended
    )
    grad_query = (grad_qu + grad_qv).astype(jnp.bfloat16)
    grad_kv = jnp.concatenate([grad_keys, grad_values], 1).astype(jnp.bfloat16)
    grad_wattn = jnp.concatenate([tdot(normed_b[MEM:], grad_query), tdot(normed_b, grad_kv)], 1)
    grad_normed = dott(grad_kv, w_attn[:, D:]) + jnp.pad(
        dott(grad_query, w_attn[:, :D]), ((MEM, 0), (0, 0))
    )
    grad_wpos = tdot(table, grad_rel.astype(jnp.bfloat16))
    grad_joined, grad_gain_one = norm_one_back(grad_normed)
    grad_hidden = grad_mixed + grad_joined[MEM:]
    grad_vectors = jnp.stack(
        [grad_gain_one, grad_gain_two, jnp.sum(grad_qu, 0), jnp.sum(grad_qv, 0)]
    )
    return (grad_hidden, (grad_wattn, grad_wout, grad_wpos, grad_up, grad_down, grad_vectors))


def head_pass(output, segment, length, target_seg, w_head, gain_final, streams):
    normed, back = jax.vjp(norm_gain, output, gain_final.astype(jnp.float32))
    normed_b = normed.astype(jnp.bfloat16)
    logits = matmul(normed_b, w_head)
    top = jnp.max(logits, -1, keepdims=True)
    log_total = top[:, 0] + jnp.log(jnp.sum(jnp.exp(logits - top), -1))
    picks = lax.broadcasted_iota(jnp.int32, logits.shape, 1) == target_seg[:, None]
    picked = jnp.sum(jnp.where(picks, logits, 0.0), -1)
    weight = row_weight(segment, length)
    term = jnp.sum((log_total - picked) * weight)
    grad_logits = (jnp.exp(logits - log_total[:, None]) - picks.astype(jnp.float32)) * (
        weight / streams
    )[:, None]
    grad_b = grad_logits.astype(jnp.bfloat16)
    grad_table = tdot(normed_b, grad_b)
    grad_output, grad_gain = back(dott(grad_b, w_head))
    return (grad_output, grad_table, grad_gain, term)


def adam_step(weight, grad, first, second, rate, decay, factor):
    grad = grad * factor
    first = 0.9 * first + 0.1 * grad
    second = 0.999 * second + 0.001 * grad * grad
    ratio = first / (1.0 - 0.9**STEP) / (jnp.sqrt(second / (1.0 - 0.999**STEP)) + 1e-08)
    return (weight - rate * (ratio + decay * weight), first, second)


def local(
    frames,
    targets,
    lengths,
    w_attn,
    w_out,
    w_pos,
    w_up,
    w_down,
    layer_vecs,
    w_in,
    w_head,
    gain_final,
    moment_attn,
    moment_out,
    moment_pos,
    moment_up,
    moment_down,
    moment_vecs,
    moment_in,
    moment_head,
    moment_final,
    second_attn,
    second_out,
    second_pos,
    second_up,
    second_down,
    second_vecs,
    second_in,
    second_head,
    second_final,
):
    section = lax.axis_index("section")
    sections = lax.axis_size("section")
    streams = lax.axis_size("dp")
    first_section = section == 0
    last_section = section == sections - 1
    gathered = (
        lax.all_gather(w_attn[0].astype(jnp.bfloat16), "dp", axis=0, tiled=True),
        lax.all_gather(w_out[0].astype(jnp.bfloat16), "dp", axis=0, tiled=True),
        lax.all_gather(w_pos[0].astype(jnp.bfloat16), "dp", axis=0, tiled=True),
        lax.all_gather(w_up[0].astype(jnp.bfloat16), "dp", axis=0, tiled=True),
        lax.all_gather(w_down[0].astype(jnp.bfloat16), "dp", axis=0, tiled=True),
        lax.all_gather(layer_vecs[0].astype(jnp.bfloat16), "dp", axis=1, tiled=True),
        lax.all_gather(w_in.astype(jnp.bfloat16), "dp", axis=1, tiled=True),
        lax.all_gather(w_head.astype(jnp.bfloat16), "dp", axis=0, tiled=True),
        lax.all_gather(gain_final.astype(jnp.bfloat16), "dp", axis=0, tiled=True),
    )
    weights = tuple(gathered[:6])
    w_in_b, w_head_b, gain_b = (gathered[6], gathered[7], gathered[8])
    frame_rows = frames[0]
    target_rows = targets[0]
    length = lengths[0]
    ticks = SEGS + sections - 1
    received = jnp.zeros((SEG, D), jnp.float32)
    previous = jnp.zeros((SEG, D), jnp.float32)
    kept = []
    for tick in range(ticks):
        micro = tick - section
        busy = (micro >= 0) & (micro < SEGS)
        if tick < SEGS:
            entry = matmul(frame_rows[tick * SEG : (tick + 1) * SEG], w_in_b)
        else:
            entry = jnp.zeros((SEG, D), jnp.float32)
        inputs = jnp.where(first_section, entry, received)
        memory = jnp.where(micro >= 1, previous[SEG - MEM :], 0.0)
        output = lax.cond(
            busy,
            lambda: layer_pass(inputs, memory, micro, length, weights)[0],
            lambda: jnp.zeros((SEG, D), jnp.float32),
        )
        kept.append(inputs)
        previous = inputs
        if tick < ticks - 1:
            received = from_behind(output, "section", 1)
    stacked = jnp.stack(kept)
    state = (
        tuple((jnp.zeros(item.shape, jnp.float32) for item in weights)),
        jnp.zeros(w_in_b.shape, jnp.float32),
        jnp.zeros(w_head_b.shape, jnp.float32),
        jnp.zeros(gain_b.shape, jnp.float32),
        jnp.zeros((), jnp.float32),
        jnp.zeros((SEG, D), jnp.float32),
    )
    grad_recv = jnp.zeros((SEG, D), jnp.float32)
    for tick in range(ticks):
        micro = SEGS - 1 - tick + (sections - 1 - section)
        busy = (micro >= 0) & (micro < SEGS)
        safe = jnp.clip(micro, 0, SEGS - 1)
        inputs = lax.dynamic_index_in_dim(stacked, safe + section, 0, keepdims=False)
        before = lax.dynamic_index_in_dim(
            stacked, jnp.maximum(safe + section - 1, 0), 0, keepdims=False
        )
        memory = jnp.where(micro >= 1, before[SEG - MEM :], 0.0)

        def work(carry):
            layer_acc, in_acc, head_acc, gain_acc, loss_acc, unused = carry
            output, saved = layer_pass(inputs, memory, safe, length, weights)
            target_seg = lax.dynamic_slice_in_dim(target_rows, safe * SEG, SEG)
            head_out = lax.cond(
                last_section,
                lambda: head_pass(output, safe, length, target_seg, w_head_b, gain_b, streams),
                lambda: (
                    jnp.zeros((SEG, D), jnp.float32),
                    jnp.zeros(w_head_b.shape, jnp.float32),
                    jnp.zeros(gain_b.shape, jnp.float32),
                    jnp.zeros((), jnp.float32),
                ),
            )
            grad_out = jnp.where(last_section, head_out[0], grad_recv)
            grad_hidden, layer_new = layer_back(saved, grad_out, weights)
            frames_seg = lax.dynamic_slice_in_dim(frame_rows, safe * SEG, SEG)
            grad_entry = jnp.where(
                first_section, tdot(frames_seg, grad_hidden.astype(jnp.bfloat16)), 0.0
            )
            return (
                tuple((a + b for a, b in zip(layer_acc, layer_new))),
                in_acc + grad_entry,
                head_acc + head_out[1],
                gain_acc + head_out[2],
                loss_acc + head_out[3],
                grad_hidden,
            )

        def rest(carry):
            return carry[:5] + (jnp.zeros((SEG, D), jnp.float32),)

        state = lax.cond(busy, work, rest, state)
        if tick < ticks - 1:
            grad_recv = from_behind(state[5], "section", -1)
    layer_grads, grad_in, grad_table, grad_gain, loss_local = (
        state[0],
        state[1],
        state[2],
        state[3],
        state[4],
    )
    dims = (0, 0, 0, 0, 0, 1, 1, 0, 0)
    summed = lax.psum(
        (
            layer_grads[0],
            layer_grads[1],
            layer_grads[2],
            layer_grads[3],
            layer_grads[4],
            layer_grads[5],
            grad_in,
            grad_table,
            grad_gain,
        ),
        "dp",
    )
    place = lax.axis_index("dp")
    shards = tuple(
        (
            lax.dynamic_slice_in_dim(
                whole, place * (whole.shape[dim] // streams), whole.shape[dim] // streams, dim
            )
            for whole, dim in zip(summed, dims)
        )
    )
    ends = lax.psum((shards[6], shards[7], shards[8]), "section")
    own_squares = jnp.zeros((), jnp.float32)
    for item in shards[:6]:
        own_squares = own_squares + jnp.sum(item * item)
    end_squares = jnp.zeros((), jnp.float32)
    for item in ends:
        end_squares = end_squares + jnp.sum(item * item)
    squares = own_squares + jnp.where(first_section, end_squares, 0.0)
    total_squares, loss_sum = lax.psum((squares, loss_local), ("section", "dp"))
    grad_norm = jnp.sqrt(total_squares)
    factor = jnp.minimum(1.0, CLIP / (grad_norm + 1e-06))
    grads = tuple(shards[:6]) + tuple(ends)
    params = (w_attn, w_out, w_pos, w_up, w_down, layer_vecs, w_in, w_head, gain_final)
    firsts = (
        moment_attn,
        moment_out,
        moment_pos,
        moment_up,
        moment_down,
        moment_vecs,
        moment_in,
        moment_head,
        moment_final,
    )
    seconds = (
        second_attn,
        second_out,
        second_pos,
        second_up,
        second_down,
        second_vecs,
        second_in,
        second_head,
        second_final,
    )
    news, moms, sqs = ([], [], [])
    for index in range(9):
        vector = index in (5, 8)
        rate = 0.3 if vector else 0.03
        decay = 0.0 if vector else 0.01
        grad = grads[index][None] if index < 6 else grads[index]
        weight, first, second = adam_step(
            params[index], grad, firsts[index], seconds[index], rate, decay, factor
        )
        news.append(weight)
        moms.append(first)
        sqs.append(second)
    return (
        news[0],
        news[1],
        news[2],
        news[3],
        news[4],
        news[5],
        news[6],
        news[7],
        news[8],
        moms[0],
        moms[1],
        moms[2],
        moms[3],
        moms[4],
        moms[5],
        moms[6],
        moms[7],
        moms[8],
        sqs[0],
        sqs[1],
        sqs[2],
        sqs[3],
        sqs[4],
        sqs[5],
        sqs[6],
        sqs[7],
        sqs[8],
        grad_norm,
        loss_sum,
    )


def solution(mesh):
    placed = (
        P("dp", None, None),
        P("dp", None),
        P("dp"),
        P("section", "dp", None),
        P("section", "dp", None),
        P("section", "dp", None),
        P("section", "dp", None),
        P("section", "dp", None),
        P("section", None, "dp"),
        P(None, "dp"),
        P("dp", None),
        P("dp"),
        P("section", "dp", None),
        P("section", "dp", None),
        P("section", "dp", None),
        P("section", "dp", None),
        P("section", "dp", None),
        P("section", None, "dp"),
        P(None, "dp"),
        P("dp", None),
        P("dp"),
        P("section", "dp", None),
        P("section", "dp", None),
        P("section", "dp", None),
        P("section", "dp", None),
        P("section", "dp", None),
        P("section", None, "dp"),
        P(None, "dp"),
        P("dp", None),
        P("dp"),
    )
    return jax.shard_map(
        local,
        mesh=mesh,
        in_specs=placed,
        out_specs=(
            P("section", "dp", None),
            P("section", "dp", None),
            P("section", "dp", None),
            P("section", "dp", None),
            P("section", "dp", None),
            P("section", None, "dp"),
            P(None, "dp"),
            P("dp", None),
            P("dp"),
            P("section", "dp", None),
            P("section", "dp", None),
            P("section", "dp", None),
            P("section", "dp", None),
            P("section", "dp", None),
            P("section", None, "dp"),
            P(None, "dp"),
            P("dp", None),
            P("dp"),
            P("section", "dp", None),
            P("section", "dp", None),
            P("section", "dp", None),
            P("section", "dp", None),
            P("section", "dp", None),
            P("section", None, "dp"),
            P(None, "dp"),
            P("dp", None),
            P("dp"),
            P(),
            P(),
        ),
        check_vma=False,
    )
```

profile of v0, /device:TPU:0, one launch (start us, length us, event | category | flops | bytes accessed | tf_op | source)
XLA Modules:
  0.0 2091.5 jit_solution(18143741147641320744)
XLA Ops:
  15.6 44.3 %all-gather = bf16[1,4,512]{1,0,2:T(2,128)(2,1)S(1)} all-gather(bf16[1,4,32]{1,0,2:T(2,128)(2,1)S(1)} %copy.363), channel_id=2, replica_groups=mesh['section'=2,'dp'=16] {'dp'}, dimensions={2}, use_global_device_ids=true | all-gather | bytes 4352 | tf_op jit(solution)/shard_map/all_gather | solution.py:331
  60.0 36.6 %all_gather.27 = bf16[80,512]{0,1:T(8,128)(2,1)S(1)} all-gather(bf16[80,32]{0,1:T(8,128)(2,1)S(1)} %convert_element_type.782), channel_id=1, replica_groups=mesh['section'=2,'dp'=16] {'dp'}, dimensions={1}, use_global_device_ids=true | all-gather | bytes 87040 | tf_op jit(solution)/shard_map/all_gather | solution.py:332
  96.7 44.8 %all-gather.2 = bf16[1,512,512]{2,1,0:T(8,128)(2,1)} all-gather(bf16[1,32,512]{2,1,0:T(8,128)(2,1)S(1)} %convert_element_type.787), channel_id=4, replica_groups=mesh['section'=2,'dp'=16] {'dp'}, dimensions={1}, use_global_device_ids=true | all-gather | bytes 557056 | tf_op jit(solution)/shard_map/all_gather | solution.py:328
  141.4 42.3 %all-gather.3 = bf16[1,512,512]{2,1,0:T(8,128)(2,1)} all-gather(bf16[1,32,512]{2,1,0:T(8,128)(2,1)S(1)} %convert_element_type.789), channel_id=5, replica_groups=mesh['section'=2,'dp'=16] {'dp'}, dimensions={1}, use_global_device_ids=true | all-gather | bytes 557056 | tf_op jit(solution)/shard_map/all_gather | solution.py:327
  185.1 19.2 all-gather.17.cloned.1.call-done
  205.2 119.0 %conditional.8 = (f32[512,512]{0,1:T(8,128)}) conditional(s32[]{:T(128)} %convert_element_type.779, () %tuple.282, (f32[256,512]{0,1:T(8,128)}, f32[512,512]{1,0:T(8,128)}, bf16[4,512]{1,0:T(4,128)(2,1)S(1)}, bf16[512,1536]{1,0:T(8,128)(2,1)}, bf16[512,512]{1,0:T(8,128)(2,1)}, /*index=5*/s32[]{:T(128)}, s32[]{:T(128)}, bf16[512,512]{1,0:T(8,128)(2,1)}, ...), branch_computations={%region_0.1_spmd, %region_1.10_spmd} | conditional | flops 4222170112 | bytes 91274320 | solution.py:354
  222.6 93.2 %while.214 = (s32[]{:T(128)}, bf16[512,512]{0,1:T(8,128)(2,1)}, bf16[768,512]{1,0:T(8,128)(2,1)}, bf16[512,512]{1,0:T(8,128)(2,1)}, bf16[768,512]{1,0:T(8,128)(2...) while((s32[]{:T(128)}, bf16[512,512]{0,1:T(8,128)(2,1)}, ...), condition=%wide.region_7.7_spmd.clone, body=%wide.region_4.6_spmd.clone.sunk | while | flops 309070336 | bytes 42163228 | solution.py:128
  231.4 6.4 reshape.1703
  254.6 6.4 reshape.1703
  277.8 6.4 reshape.1703
  301.0 6.4 reshape.1703
  318.2 5.8 fusion.47
  330.7 118.4 %conditional.9 = (f32[512,512]{0,1:T(8,128)}) conditional(s32[]{:T(128)} %convert_element_type.780, () %tuple.284, (pred[]{:T(512)}, f32[512,512]{1,0:T(8,128)}, f32[256,512]{0,1:T(8,128)}, f32[512,512]{1,0:T(8,128)}, bf16[4,512]{1,0:T(4,128)(2,1)S(1)}, /*index=5*/bf16[512,1536]{1,0:T(8,128)(2,1)}, bf16[512,512]{1,0:T(8,128)(2,1)}, s32[]{:T(128)}, ...), branch_computations={%region_10.11_spmd, %region_11.20_spmd} | conditional | flops 4222301184 | bytes 94944336 | solution.py:354
  347.4 93.5 %while.215 = (s32[]{:T(128)}, bf16[512,512]{0,1:T(8,128)(2,1)}, bf16[768,512]{1,0:T(8,128)(2,1)}, bf16[512,512]{1,0:T(8,128)(2,1)}, bf16[768,512]{1,0:T(8,128)(2...) while((s32[]{:T(128)}, bf16[512,512]{0,1:T(8,128)(2,1)}, ...), condition=%wide.region_17.17_spmd.clone, body=%wide.region_14.16_spmd.clone.sunk | while | flops 309070336 | bytes 42163228 | solution.py:128
  356.6 6.4 reshape.1702
  379.8 6.4 reshape.1702
  403.0 6.4 reshape.1702
  426.2 6.4 reshape.1702
  443.4 5.7 fusion.91
  456.4 40.0 %all-reduce.14 = bf16[512]{0:T(512)(128)(2,1)} all-reduce(bf16[512]{0:T(512)(128)(2,1)S(1)} %dynamic-update-slice), channel_id=1, replica_groups=mesh['section'=2,'dp'=16] {'dp'}, use_global_device_ids=true, to_apply=%add.14 | all-reduce | flops 512 | bytes 2048
  500.0 17.5 conditional.10
  518.9 328.3 %collective-permute-done.2 = f32[512,512]{0,1:T(8,128)} collective-permute-done((f32[512,512]{0,1:T(8,128)}, f32[512,512]{0,1:T(8,128)}, u32[]{:S(2)}, u32[]{:S(2)}) %collective-permute-start.2) | collective-permute-done | bytes 1048608 | tf_op jit(solution)/shard_map/ppermute | solution.py:22
  847.2 353.1 %conditional.11 = (f32[512,1536]{1,0:T(8,128)}, f32[512,512]{1,0:T(8,128)}, f32[512,512]{1,0:T(8,128)}, f32[512,2048]{1,0:T(8,128)}, f32[2048,512]{1,0:T(8,128)}...) conditional(s32[]{:T(128)} %convert_element_type.780, ...), branch_computations={%region_52.53_spmd, %region_53.84_spmd} | conditional | flops 14247966720 | bytes 461214144 | solution.py:415
  871.8 90.3 %while.218 = (s32[]{:T(128)}, bf16[512,512]{0,1:T(8,128)(2,1)}, f32[8,512]{1,0:T(8,128)}, bf16[768,512]{0,1:T(8,128)(2,1)}, bf16[512,512]{0,1:T(8,128)(2,1)}, /*...) while((s32[]{:T(128)}, bf16[512,512]{0,1:T(8,128)(2,1)}, ...), condition=%wide.region_59.59_spmd.clone, body=%wide.region_56.58_spmd.clone.sunk | while | flops 309853184 | bytes 40487056 | solution.py:128
  880.2 6.4 reshape.1694
  902.7 6.4 reshape.1694
  925.1 6.4 reshape.1694
  947.5 6.4 reshape.1694
  970.4 4.2 add.1542
  980.3 6.3 convolution_add_fusion.3
  987.8 5.5 convolution_add_fusion.4
  1005.6 177.8 %while.219 = (s32[]{:T(128)}, f32[512,512]{0,1:T(8,128)}, f32[512,512]{0,1:T(8,128)}, bf16[768,512]{0,1:T(8,128)(2,1)}, bf16[768,512]{0,1:T(8,128)(2,1)}, /*inde...) while((s32[]{:T(128)}, f32[512,512]{0,1:T(8,128)}, ...), condition=%wide.region_77.77_spmd.clone, body=%wide.region_75.76_spmd.clone.sunk | while | flops 915408640 | bytes 84317568 | solution.py:167
  1017.6 6.4 reshape.1695
  1031.4 4.1 multiply_convert_fusion.54
  1061.9 6.4 reshape.1695
  1075.7 4.1 multiply_convert_fusion.54
  1106.2 6.4 reshape.1695
  1120.0 4.1 multiply_convert_fusion.54
  1150.5 6.4 reshape.1695
  1164.3 4.1 multiply_convert_fusion.54
  1196.2 4.1 maximum_add_fusion
  1201.6 10.9 collective-permute-done.3
  1212.5 352.0 %conditional.12 = ((f32[512,1536]{1,0:T(8,128)}, f32[512,512]{1,0:T(8,128)}, f32[512,512]{1,0:T(8,128)}, f32[512,2048]{1,0:T(8,128)}, f32[2048,512]{1,0:T(8,128)...) conditional(s32[]{:T(128)} %convert_element_type.779, ...), branch_computations={%region_84.85_spmd, %region_85.116_spmd} | conditional | flops 14247966720 | bytes 459110784 | solution.py:415
  1237.1 90.4 %while.220 = (s32[]{:T(128)}, bf16[512,512]{0,1:T(8,128)(2,1)}, f32[8,512]{1,0:T(8,128)}, bf16[768,512]{0,1:T(8,128)(2,1)}, bf16[512,512]{0,1:T(8,128)(2,1)}, /*...) while((s32[]{:T(128)}, bf16[512,512]{0,1:T(8,128)(2,1)}, ...), condition=%wide.region_91.91_spmd.clone, body=%wide.region_88.90_spmd.clone.sunk | while | flops 309853184 | bytes 40483948 | solution.py:128
  1245.4 6.4 reshape.1690
  1267.8 6.4 reshape.1690
  1290.2 6.4 reshape.1690
  1312.7 6.4 reshape.1690
  1335.8 4.2 add.1597
  1345.7 6.3 convolution_add_fusion.8
  1353.3 5.5 convolution_add_fusion.9
  1371.0 177.8 %while.221 = (s32[]{:T(128)}, f32[512,512]{0,1:T(8,128)}, f32[512,512]{0,1:T(8,128)}, bf16[768,512]{0,1:T(8,128)(2,1)}, bf16[768,512]{0,1:T(8,128)(2,1)}, /*inde...) while((s32[]{:T(128)}, f32[512,512]{0,1:T(8,128)}, ...), condition=%wide.region_109.109_spmd.clone, body=%wide.region_107.108_spmd.clone.sunk | while | flops 915408640 | bytes 84317568 | solution.py:167
  1382.9 6.4 reshape.1691
  1396.6 4.1 multiply_convert_fusion.53
  1427.2 6.4 reshape.1691
  1441.0 4.1 multiply_convert_fusion.53
  1471.5 6.4 reshape.1691
  1485.3 4.1 multiply_convert_fusion.53
  1515.9 6.4 reshape.1691
  1529.7 4.1 multiply_convert_fusion.53
  1560.2 4.1 maximum_add_fusion.2
  1567.0 76.1 %all-reduce.16 = (f32[4,512]{1,0:T(4,128)S(1)}, f32[512]{0:T(512)S(1)}) all-reduce(f32[4,512]{1,0:T(4,128)S(1)} %copy-done.160, f32[512]{0:T(512)S(1)} %copy-done.198), channel_id=1, replica_groups=mesh['section'=2,'dp'=16] {'dp'}, use_global_device_ids=true, to_apply=%region_126.127 | all-reduce | flops 2560 | bytes 20480 | tf_op jit(solution)/shard_map/psum | solution.py:426
  1643.8 364.0 %all-reduce.24.cloned.1.call-done = (f32[512,1536]{1,0:T(8,128)}, f32[512,512]{1,0:T(8,128)}, f32[512,512]{1,0:T(8,128)}, f32[512,2048]{1,0:T(8,128)}, f32[2048,...) async-done(((f32[512,1536]{1,0:T(8,128)}, f32[512,512]{1,0:T(8,128)}, f32[512,512]{1,0:T(8,128)}, f32[512,2048]{1,0:T(8,128)}, f32[2048,512]{1,0:T(8,128)}, ...) | async-done | bytes 15892496 | tf_op jit(solution)/shard_map/psum | solution.py:426
  2030.7 41.2 %all-reduce.15 = (f32[]{:T(128)}, f32[]{:T(128)}) all-reduce(f32[]{:T(128)S(6)} %add.1665, f32[]{:T(128)} %get-tuple-element.3201), channel_id=1, replica_groups=mesh['section'=2,'dp'=16] {'section','dp'}, use_global_device_ids=true, to_apply=%region_137.138 | all-reduce | flops 2 | bytes 16 | tf_op jit(solution)/shard_map/psum | solution.py:457
  (1203 shorter events, 773.0 us)
Async XLA Ops:
  7.2 176.6 %copy-start.135 = (bf16[1,1024,80]{1,2,0:T(8,128)(2,1)S(1)}, bf16[1,1024,80]{1,2,0:T(8,128)(2,1)}, u32[]{:S(2)}) copy-start(bf16[1,1024,80]{1,2,0:T(8,128)(2,1)} %param.62) | copy-start | bytes 491524
  7.2 177.9 %all-gather.13.cloned.1.call-start = ((), (), s32[]{:S(2)}) async-start(), calls=%async_computation.2 | async-start | bytes 1671168 | tf_op jit(solution)/shard_map/all_gather | solution.py:326
  8.9 176.2 %all-gather.15.cloned.1.call-start = ((), (), s32[]{:S(2)}) async-start(), calls=%async_computation.3 | async-start | bytes 2228224 | tf_op jit(solution)/shard_map/all_gather | solution.py:329
  10.6 193.7 %all-gather.17.cloned.1.call-start = ((), (), s32[]{:S(2)}) async-start(), calls=%async_computation.4 | async-start | bytes 2228224 | tf_op jit(solution)/shard_map/all_gather | solution.py:330
  12.3 486.0 %all-gather.11.cloned.1.call-start = ((), (), s32[]{:S(2)}) async-start(), calls=%async_computation | async-start | bytes 1114112 | tf_op jit(solution)/shard_map/all_gather | solution.py:333
  96.7 87.1 %copy-start.124 = (bf16[80,512]{0,1:T(8,128)(2,1)}, bf16[80,512]{0,1:T(8,128)(2,1)S(1)}, u32[]{:S(2)}) copy-start(bf16[80,512]{0,1:T(8,128)(2,1)S(1)} %all_gather.27) | copy-start | bytes 245764
  324.2 5.2 copy-start.125
  324.2 5.2 copy-start.136
  325.8 3.6 collective-permute-start
  327.9 1679.9 %all-reduce.24.cloned.1.call-start = ((), (), s32[]{:S(2)}) async-start(), calls=%async_computation.5 | async-start | bytes 31981568 | tf_op jit(solution)/shard_map/psum | solution.py:426
  449.1 5.8 copy-start.225
  449.1 5.8 copy-start.234
  450.7 45.7 %collective-permute-start.1 = (f32[512,512]{1,0:T(8,128)S(1)}, f32[512,512]{1,0:T(8,128)S(1)}, u32[]{:S(2)}, u32[]{:S(2)}) collective-permute-start(f32[512,512]{1,0:T(8,128)S(1)} %copy.369), channel_id=1, source_target_pairs={{0,16},{1,17},{2,18},{3,19},{4,20},{5,21},{6,22},{7,23},{8,24},{9,... | collective-permute-start | bytes 3145736 | tf_op jit(solution)/shard_map/ppermute | solution.py:22
  517.6 329.6 %copy-start.155 = (f32[4,512]{1,0:T(4,128)}, f32[4,512]{1,0:T(4,128)S(1)}, u32[]{:S(2)}) copy-start(f32[4,512]{1,0:T(4,128)S(1)} %get-tuple-element.3175) | copy-start | bytes 24580
  517.6 329.6 %collective-permute-start.2 = (f32[512,512]{0,1:T(8,128)}, f32[512,512]{0,1:T(8,128)}, u32[]{:S(2)}, u32[]{:S(2)}) collective-permute-start(f32[512,512]{0,1:T(8,128)} %get-tuple-element.3180), channel_id=1, source_target_pairs={{16,0},{17,1},{18,2},{19,3},{20,4},{21,5},{22,6},{23,7},{24,8},{25... | collective-permute-start | bytes 3145736 | tf_op jit(solution)/shard_map/ppermute | solution.py:22
  848.5 15.3 copy-start.203
  853.4 5.0 copy-start.4
  970.4 5.8 copy-start.96
  974.7 5.6 copy-start.195
  980.3 6.3 copy-start.47
  1000.5 5.1 copy-start.166
  1009.3 5.7 copy-start.67
  1053.6 5.7 copy-start.67
  1097.9 5.7 copy-start.67
  1142.2 5.7 copy-start.67
  1200.3 12.2 collective-permute-start.3
  1213.8 15.4 copy-start.201
  1218.7 5.0 copy-start.5
  1335.8 5.8 copy-start.98
  1340.1 5.6 copy-start.197
  1345.7 6.3 copy-start.49
  1374.5 5.7 copy-start.69
  1418.9 5.7 copy-start.69
  1463.2 5.7 copy-start.69
  1507.6 5.7 copy-start.69
  1566.3 506.3 %copy-start.126 = (f32[1,128,512]{2,1,0:T(8,128)S(1)}, f32[1,128,512]{2,1,0:T(8,128)}, u32[]{:S(2)}) copy-start(f32[1,128,512]{2,1,0:T(8,128)} %param.69) | copy-start | bytes 786436
  1566.3 506.3 %copy-start.143 = (f32[1,128,512]{2,1,0:T(8,128)S(1)}, f32[1,128,512]{2,1,0:T(8,128)}, u32[]{:S(2)}) copy-start(f32[1,128,512]{2,1,0:T(8,128)} %param.78) | copy-start | bytes 786436
  1566.3 506.3 %copy-start.144 = (f32[1,128,512]{2,1,0:T(8,128)S(1)}, f32[1,128,512]{2,1,0:T(8,128)}, u32[]{:S(2)}) copy-start(f32[1,128,512]{2,1,0:T(8,128)} %param.87) | copy-start | bytes 786436
  1566.3 508.4 %copy-start.127 = (f32[1,32,2048]{2,1,0:T(8,128)S(1)}, f32[1,32,2048]{2,1,0:T(8,128)}, u32[]{:S(2)}) copy-start(f32[1,32,2048]{2,1,0:T(8,128)} %param.68) | copy-start | bytes 786436
  1566.3 508.4 %copy-start.145 = (f32[1,32,2048]{2,1,0:T(8,128)S(1)}, f32[1,32,2048]{2,1,0:T(8,128)}, u32[]{:S(2)}) copy-start(f32[1,32,2048]{2,1,0:T(8,128)} %param.77) | copy-start | bytes 786436
  1566.4 508.4 %copy-start.146 = (f32[1,32,2048]{2,1,0:T(8,128)S(1)}, f32[1,32,2048]{2,1,0:T(8,128)}, u32[]{:S(2)}) copy-start(f32[1,32,2048]{2,1,0:T(8,128)} %param.86) | copy-start | bytes 786436
  1566.4 460.8 %all-reduce.22.cloned.1.call-start = ((), (), s32[]{:S(2)}) async-start(), calls=%async_computation.1 | async-start | bytes 262144 | tf_op jit(solution)/shard_map/psum | solution.py:449
  2022.2 54.8 %copy-start.128 = (f32[1,32,1536]{2,1,0:T(8,128)S(1)}, f32[1,32,1536]{2,1,0:T(8,128)}, u32[]{:S(2)}) copy-start(f32[1,32,1536]{2,1,0:T(8,128)} %param.65) | copy-start | bytes 589828
  2022.2 54.8 %copy-start.149 = (f32[1,32,1536]{2,1,0:T(8,128)S(1)}, f32[1,32,1536]{2,1,0:T(8,128)}, u32[]{:S(2)}) copy-start(f32[1,32,1536]{2,1,0:T(8,128)} %param.74) | copy-start | bytes 589828
  2022.2 54.8 %copy-start.150 = (f32[1,32,1536]{2,1,0:T(8,128)S(1)}, f32[1,32,1536]{2,1,0:T(8,128)}, u32[]{:S(2)}) copy-start(f32[1,32,1536]{2,1,0:T(8,128)} %param.83) | copy-start | bytes 589828
  2072.6 6.2 copy-start.215
  2072.6 6.2 copy-start.218
  2072.6 6.2 copy-start.219
  2072.7 6.8 copy-start.226
  2072.7 6.8 copy-start.227
  2072.7 6.8 copy-start.228
  2072.7 7.4 copy-start.174
  2072.7 7.3 copy-start.207
  2072.7 7.3 copy-start.208
  2074.7 6.0 copy-start.147
  2074.7 6.0 copy-start.148
  2074.8 5.9 copy-start.170
  2074.8 5.9 copy-start.171
  2074.8 5.9 copy-start.172
  2074.8 5.9 copy-start.173
  2074.8 7.6 copy-start.139
  2074.8 7.6 copy-start.140
  2074.8 7.6 copy-start.153
  2074.8 7.6 copy-start.154
  (213 other events, 495.4 us)
Sparse Core Ops, SparseCore 0:
  11.4 61.7 all-gather.12
  76.5 63.4 all-gather.14
  143.4 60.8 all-gather.16
  328.0 53.9 all-gather.10
  1566.5 441.2 all-reduce.23
  2010.5 16.6 all-reduce.21
where the time goes:
time: 2110 us; the launch traced here: 2090 us
  waiting for transfers between devices  725 us (34%)
  local copies, waits for them, and re-layouts  630 us (30%)
  blocking collectives  329 us (16%)
  matrix products  243 us (12%)
  other arithmetic  121 us (6%)
  between operations  23.4 us (1%)
    psum x1, waiting for transfers between devices, local(): lax.psum((layer_grads[0], layer_grads[1], layer_grads[2], layer_grads[3],...  364 us
    ppermute x4, waiting for transfers between devices, from_behind(): lax.ppermute(value, axis, [(source, source + steps) for source in range(i...  341 us
    reshape x24, local copies, waits for them, and re-layouts, skew(): jnp.pad(block, ((0, 0), (0, 0), (0, 1))).reshape(count, rows * (cols + 1))  154 us
    dynamic_slice x144, local copies, waits for them, and re-layouts, slab(): lax.dynamic_slice_in_dim(block, pair * width, width, 1)  142 us
    dot_general x104, matrix products, einmul(): return jnp.einsum(form, left, right, preferred_element_type=jnp.float32)  102 us
    slice x24, local copies, waits for them, and re-layouts, skew(): return flat[:, lead:lead + rows * cols].reshape(count, rows, cols)  83.6 us
    psum x1, blocking collectives, local(): lax.psum((layer_grads[0], layer_grads[1], layer_grads[2], layer_grads[3],...  76.1 us
    pad x24, local copies, waits for them, and re-layouts, skew(): jnp.pad(block, ((0, 0), (0, 0), (0, 1))).reshape(count, rows * (cols + 1))  48.9 us
  transfers between devices with their start and end apart: 10, of which 6 were waited for; matrix products, arithmetic and copies ran while one was open for 7% of the time, Pallas kernels for 0%

commit v1 on v0

v1 whole, which is shorter than its diff:
```python
import functools

import jax
import jax.numpy as jnp
from jax import lax
from jax.experimental import pallas as pl
from jax.experimental.pallas import tpu as pltpu
from jax.sharding import PartitionSpec as P

D = 512
FF = 2048
CODES = 1024
FEATS = 80
MEM = 256
SEG = 512
SEGS = 2
STEP = 10
ROWS = MEM + SEG
BLOCK = 128
PAIRS = 4
WIDE = 18 * BLOCK
GROUPS = 16
NEG = -1e30
CLIP = 0.02
SCALE = 0.125
F32 = jnp.float32
BF16 = jnp.bfloat16
SPANS = tuple((MEM + BLOCK * (b + 1) for b in range(4)))
STARTS = tuple((sum(SPANS[:b]) for b in range(4)))
VMEM_LIMIT = 56 * 1024 * 1024


def nn(left, right):
    return jnp.dot(left, right, preferred_element_type=F32)


def nt(left, right):
    return lax.dot_general(left, right, (((1,), (1,)), ((), ())), preferred_element_type=F32)


def tn(left, right):
    return lax.dot_general(left, right, (((0,), (0,)), ((), ())), preferred_element_type=F32)


def norm_parts(values):
    center = values - jnp.mean(values, -1, keepdims=True)
    spread = jnp.mean(center * center, -1, keepdims=True)
    inverse = lax.rsqrt(spread + 1e-05)
    return center * inverse, inverse


def norm_back(unit, inverse, gain, grad):
    scaled = grad * gain
    first = jnp.mean(scaled, -1, keepdims=True)
    second = jnp.mean(scaled * unit, -1, keepdims=True)
    return inverse * (scaled - first - unit * second), jnp.sum(grad * unit, 0, keepdims=True)


def group_of(bits, spot, place, half):
    code = jnp.int32(0)
    for index, (low, high) in enumerate(zip(bits[0], bits[1])):
        bit = lax.rem(lax.div(spot, 1 << index), 2)
        code = code + bit * jnp.where(half == 0, low, high)
    return jnp.bitwise_xor(place, code)


def copies(bits, place, half, pieces, units, rows, sem, outward):
    count = GROUPS // len(pieces)
    for index, slab in enumerate(pieces):

        def one(spot, carry):
            group = group_of(bits, index * count + spot, place, half)
            for whole, first in units:
                there = whole.at[pl.ds(pl.multiple_of((group * 2 + half) * rows, rows), rows), :]
                here = slab.at[spot, pl.ds(first, rows), pl.ds(0, whole.shape[1])]
                if outward:
                    pltpu.make_async_copy(there, here, sem).start()
                else:
                    pltpu.make_async_copy(here, there, sem).start()
            return carry

        lax.fori_loop(0, count, one, 0)


def tri_mask():
    row = lax.broadcasted_iota(jnp.int32, (2 * BLOCK, BLOCK), 0)
    col = lax.broadcasted_iota(jnp.int32, (2 * BLOCK, BLOCK), 1)
    return col <= lax.rem(row, BLOCK)


def stack_heads(part):
    col = lax.broadcasted_iota(jnp.int32, part.shape, 1)
    zero = jnp.zeros_like(part)
    return jnp.concatenate(
        [jnp.where(col < 64, part, zero), jnp.where(col < 64, zero, part)], 0
    )


def pick_heads(both):
    col = lax.broadcasted_iota(jnp.int32, (BLOCK, BLOCK), 1)
    return jnp.where(col < 64, both[:BLOCK], both[BLOCK:])


def lanes(pair):
    return pl.ds(pl.multiple_of(pair * BLOCK, BLOCK), BLOCK)


def attn_forward(bits, base, *refs):
    first_layer = base == 0
    if first_layer:
        (scalars, frames, own_low, own_high, other_low, other_high, table, mixed, joined, normed,
         query_u, query_v, keys, values, rel, probs, attended, weights, vecs, sem, small,
         small_sem) = refs
    else:
        (scalars, memory, hidden, vecs, own_low, own_high, other_low, other_high, table, mixed,
         joined, normed, query_u, query_v, keys, values, rel, probs, attended, weights, sem) = refs
    place, half, length, segment = scalars[0], scalars[1], scalars[2], scalars[3]
    both = ((half, (own_low, own_high)), (1 - half, (other_low, other_high)))
    if first_layer:
        for which, pieces in both:
            copies(bits, place, which, pieces, [(small, 80)], 16, small_sem, False)
    units = [(weights.at[u], 16 * u) for u in range(5)]
    for which, pieces in both:
        copies(bits, place, which, pieces, units, 16, sem, False)
    if first_layer:
        pltpu.make_async_copy(small, small, small_sem).wait()
        vecs[...] = jnp.transpose(small[...].astype(F32))[80:96]
        for b in range(3):
            rows = pl.ds(256 * b, 256)
            joined[rows, :] = nt(frames[rows, :], small[...])
    else:
        joined[0:MEM, :] = memory[...]
        joined[MEM:, :] = hidden[...]
    gain = vecs[base : base + 1, :]
    bias_u = vecs[base + 2 : base + 3, :]
    bias_v = vecs[base + 3 : base + 4, :]
    for b in range(3):
        rows = pl.ds(256 * b, 256)
        unit, unused = norm_parts(joined[rows, :])
        normed[rows, :] = (unit * gain).astype(BF16)
    pltpu.make_async_copy(weights, weights, sem).wait()
    for b in range(3):
        rows = pl.ds(256 * b, 256)
        part = normed[rows, :]
        keys[rows, :] = nn(part, weights[1]).astype(BF16)
        values[rows, :] = nn(part, weights[2]).astype(BF16)
        rel[rows, :] = nn(table[rows, :], weights[4]).astype(BF16)
        if b > 0:
            query = nn(part, weights[0])
            back = pl.ds(256 * (b - 1), 256)
            query_u[back, :] = (query + bias_u).astype(BF16)
            query_v[back, :] = (query + bias_v).astype(BF16)
    spot = lax.broadcasted_iota(jnp.int32, (1, ROWS), 1)
    where_at = segment * SEG + spot - MEM
    allowed = (where_at < length) & ((spot >= MEM) | (segment >= 1))
    bias = jnp.where(allowed, 0.0, NEG)
    triangle = tri_mask()

    def one_pair(pair, carry):
        lane = lanes(pair)
        for b, span in enumerate(SPANS):
            rows = pl.ds(BLOCK * b, BLOCK)
            stack_u = stack_heads(query_u[rows, lane]) * SCALE
            stack_v = stack_heads(query_v[rows, lane]) * SCALE
            content = nt(stack_u, keys[0:span, lane])
            full = nt(stack_v, rel[ROWS - span : ROWS, lane])
            position = jnp.concatenate(
                [
                    pltpu.roll(full[:BLOCK], span - BLOCK + 1, 1, stride=1, stride_axis=0),
                    pltpu.roll(full[BLOCK:], span - BLOCK + 1, 1, stride=1, stride_axis=0),
                ],
                0,
            )
            score = content + position + bias[:, :span]
            score = jnp.concatenate(
                [score[:, : span - BLOCK], jnp.where(triangle, score[:, span - BLOCK :], NEG)], 1
            )
            top = jnp.max(score, -1, keepdims=True)
            expo = jnp.exp(score - top)
            total = jnp.sum(expo, -1, keepdims=True)
            prob = (expo * (1.0 / total)).astype(BF16)
            probs[pair, :, STARTS[b] : STARTS[b] + span] = prob
            attended[rows, lane] = pick_heads(nn(prob, values[0:span, lane])).astype(BF16)
        return carry

    lax.fori_loop(0, PAIRS, one_pair, 0)
    for b in range(2):
        rows = pl.ds(256 * b, 256)
        mixed[rows, :] = joined[pl.ds(MEM + 256 * b, 256), :] + nn(attended[rows, :], weights[3])


def attn_backward(bits, base, *refs):
    last_kernel = base == 0
    (scalars, grad_mixed, joined, normed, query_u, query_v, keys, values, rel, probs, attended,
     weights, vecs, table) = refs[:14]
    if last_kernel:
        (frames, gain_two, vecs_one, gain_two_one, gain_final, keep, send) = refs[14:21]
        (staged_small, small_sem) = refs[-2:]
        rest = refs[21:-2]
    else:
        (keep, send, grad_hidden, grad_vecs) = refs[14:18]
        rest = refs[18:]
    (flip, grad_att, acc_keys, acc_values, acc_rel, grad_qu, grad_qv, staged, smalls, sem) = rest
    place, half = scalars[0], scalars[1]
    row = lax.broadcasted_iota(jnp.int32, (2 * BLOCK, 2 * BLOCK), 0)
    col = lax.broadcasted_iota(jnp.int32, (2 * BLOCK, 2 * BLOCK), 1)
    back = (row // BLOCK) * BLOCK + BLOCK - 1 - lax.rem(row, BLOCK)
    flip[...] = (col == back).astype(F32).astype(BF16)
    grad_mixed_b = grad_mixed[...].astype(BF16)
    staged[3] = tn(attended[...], grad_mixed_b).astype(BF16)
    grad_att[...] = nt(grad_mixed_b, weights[3]).astype(BF16)

    def one_pair(pair, carry):
        lane = lanes(pair)
        for b in (3, 2, 1, 0):
            span = SPANS[b]
            rows = pl.ds(BLOCK * b, BLOCK)
            stack_u = stack_heads(query_u[rows, lane]) * SCALE
            stack_v = nn(flip[...], stack_heads(query_v[rows, lane]) * SCALE).astype(BF16)
            stack_g = stack_heads(grad_att[rows, lane])
            prob_b = probs[pair, :, STARTS[b] : STARTS[b] + span]
            prob = prob_b.astype(F32)
            grad_prob = nt(stack_g, values[0:span, lane])
            inner = jnp.sum(prob * grad_prob, -1, keepdims=True)
            grad_score = (prob * (grad_prob - inner)).astype(BF16)
            turned = nn(flip[...], grad_score)
            grad_full = jnp.concatenate(
                [
                    pltpu.roll(turned[:BLOCK], 0, 1, stride=1, stride_axis=0),
                    pltpu.roll(turned[BLOCK:], 0, 1, stride=1, stride_axis=0),
                ],
                0,
            ).astype(BF16)
            grad_qu[rows, lane] = pick_heads(nn(grad_score, keys[0:span, lane])) * SCALE
            grad_qv[rows, lane] = pick_heads(nn(grad_full, rel[ROWS - span : ROWS, lane])) * SCALE
            part_keys = tn(stack_u, grad_score)
            part_values = tn(stack_g, prob_b)
            part_rel = tn(stack_v, grad_full)
            if b == 3:
                acc_keys[lane, :] = part_keys
                acc_values[lane, :] = part_values
                acc_rel[lane, :] = part_rel
            else:
                acc_keys[lane, 0:span] += part_keys
                acc_values[lane, 0:span] += part_values
                acc_rel[lane, ROWS - span : ROWS] += part_rel
        return carry

    lax.fori_loop(0, PAIRS, one_pair, 0)
    sum_u = jnp.sum(grad_qu[...], 0, keepdims=True)
    sum_v = jnp.sum(grad_qv[...], 0, keepdims=True)
    flip_one = flip[0:BLOCK, 0:BLOCK]
    turned = []
    for b in range(4):
        rows = pl.ds(BLOCK * b, BLOCK)
        part = grad_qv[rows, :]
        high = part.astype(BF16)
        low = (part - high.astype(F32)).astype(BF16)
        turned.append((grad_qu[rows, :] + nn(flip_one, high) + nn(flip_one, low)).astype(BF16))
    grad_query = jnp.concatenate(turned, 0)
    grad_keys = jnp.transpose(acc_keys[...]).astype(BF16)
    grad_values = jnp.transpose(acc_values[...]).astype(BF16)
    grad_rel = jnp.transpose(acc_rel[...]).astype(BF16)
    staged[0] = tn(normed[MEM:, :], grad_query).astype(BF16)
    staged[1] = tn(normed[...], grad_keys).astype(BF16)
    staged[2] = tn(normed[...], grad_values).astype(BF16)
    staged[4] = tn(table[...], grad_rel).astype(BF16)
    units = [(staged.at[u], 16 * u) for u in range(5)]
    copies(bits, place, half, (keep,), units, 16, sem, True)
    copies(bits, place, 1 - half, (send,), units, 16, sem, True)
    gain = vecs[base : base + 1, :]
    grad_normed = nt(grad_keys, weights[1]) + nt(grad_values, weights[2])
    unit, inverse = norm_parts(joined[0:MEM, :])
    unused, grad_gain = norm_back(unit, inverse, gain, grad_normed[0:MEM])
    unit, inverse = norm_parts(joined[MEM:, :])
    grad_here = grad_normed[MEM:] + nt(grad_query, weights[0])
    grad_joined, grad_gain_here = norm_back(unit, inverse, gain, grad_here)
    grad_gain = grad_gain + grad_gain_here
    grad_in = grad_mixed[...] + grad_joined
    if last_kernel:
        entry = tn(frames[MEM:, :], grad_in.astype(BF16))
        smalls[...] = entry
        smalls[80:81, :] = grad_gain
        smalls[81:82, :] = gain_two[0:1, :]
        smalls[82:83, :] = sum_u
        smalls[83:84, :] = sum_v
        smalls[84:88, :] = vecs_one[0:4, :]
        smalls[85:86, :] = gain_two_one[0:1, :]
        smalls[88:89, :] = gain_final[0:1, :]
        staged_small[...] = jnp.zeros_like(staged_small)
        staged_small[:, 0:BLOCK] = jnp.transpose(smalls[...]).astype(BF16)
        units = [(staged_small, 80)]
        copies(bits, place, half, (keep,), units, 16, small_sem, True)
        copies(bits, place, 1 - half, (send,), units, 16, small_sem, True)
        pltpu.make_async_copy(staged_small, staged_small, small_sem).wait()
    else:
        grad_hidden[...] = grad_in
        grad_vecs[...] = jnp.zeros_like(grad_vecs)
        grad_vecs[0:1, :] = grad_gain
        grad_vecs[2:3, :] = sum_u
        grad_vecs[3:4, :] = sum_v
    pltpu.make_async_copy(staged, staged, sem).wait()


def feed_forward(bits, base, scalars, mixed, vecs, own_low, own_high, other_low, other_high, output, normed, active, slope, up, down, sem):
    place, half = scalars[0], scalars[1]
    ups = [(up.at[u], 16 * u) for u in range(4)]
    downs = [(down, 64)]
    for which, pieces in ((half, (own_low, own_high)), (1 - half, (other_low, other_high))):
        copies(bits, place, which, pieces, ups, 16, sem.at[0], False)
        copies(bits, place, which, pieces, downs, 64, sem.at[1], False)
    gain = vecs[base + 1 : base + 2, :]
    for b in range(2):
        rows = pl.ds(256 * b, 256)
        unit, unused = norm_parts(mixed[rows, :])
        normed[rows, :] = (unit * gain).astype(BF16)
    pltpu.make_async_copy(up, up, sem.at[0]).wait()
    for b in range(2):
        rows = pl.ds(256 * b, 256)
        for u in range(4):
            inner = nn(normed[rows, :], up[u])
            square = inner * inner
            bent = jnp.tanh(0.7978845608028654 * (inner + 0.044715 * (square * inner)))
            part = 0.5 * (1.0 + bent)
            active[rows, 512 * u : 512 * (u + 1)] = (inner * part).astype(BF16)
            slope[rows, 512 * u : 512 * (u + 1)] = (
                part
                + (0.5 * inner)
                * (1.0 - bent * bent)
                * (0.7978845608028654 * (1.0 + (3 * 0.044715) * square))
            ).astype(BF16)
    pltpu.make_async_copy(down, down, sem.at[1]).wait()
    for b in range(2):
        rows = pl.ds(256 * b, 256)
        output[rows, :] = mixed[rows, :] + nn(active[rows, :], down[...])


def feed_backward(bits, base, scalars, grad_out, mixed, vecs, normed, active, slope, up, down,
                  keep, send, grad_mixed, grad_gain, grad_inner, staged_up, staged_down, sem):
    place, half = scalars[0], scalars[1]
    grad_y = grad_out[...].astype(BF16)
    for u in range(4):
        cols = slice(512 * u, 512 * (u + 1))
        part = nt(grad_y, down[cols, :])
        grad_inner[:, cols] = (part * slope[:, cols].astype(F32)).astype(BF16)
        staged_down[cols, :] = tn(active[:, cols], grad_y).astype(BF16)
        staged_up[u] = tn(normed[...], grad_inner[:, cols]).astype(BF16)
    ups = [(staged_up.at[u], 16 * u) for u in range(4)]
    downs = [(staged_down, 64)]
    for which, pieces in ((half, (keep,)), (1 - half, (send,))):
        copies(bits, place, which, pieces, ups, 16, sem.at[0], True)
        copies(bits, place, which, pieces, downs, 64, sem.at[1], True)
    grad_normed = nt(grad_inner[:, 0:512], up[0])
    for u in range(1, 4):
        grad_normed = grad_normed + nt(grad_inner[:, 512 * u : 512 * (u + 1)], up[u])
    unit, inverse = norm_parts(mixed[...])
    grad_here, gains = norm_back(unit, inverse, vecs[base + 1 : base + 2, :], grad_normed)
    grad_mixed[...] = grad_out[...] + grad_here
    grad_gain[...] = jnp.broadcast_to(gains, grad_gain.shape)
    pltpu.make_async_copy(staged_up, staged_up, sem.at[0]).wait()
    pltpu.make_async_copy(staged_down, staged_down, sem.at[1]).wait()


def head_pass(bits, streams, scalars, output, targets, vecs, own_low, own_high, other_low, other_high,
              keep, send, grad_out, grad_gain, loss, table, final, grad_logits, staged, sem):
    place, half, length, segment = scalars[0], scalars[1], scalars[2], scalars[3]
    units = [(table.at[u], 128 + 16 * u) for u in range(2)]
    copies(bits, place, half, (own_low, own_high), units, 16, sem, False)
    copies(bits, place, 1 - half, (other_low, other_high), units, 16, sem, False)
    pltpu.make_async_copy(table, table, sem).wait()
    size = length.astype(F32)
    gain = vecs[8:9, :]
    gains = jnp.zeros((1, D), F32)
    terms = jnp.zeros((1, 1), F32)
    for b in range(2):
        rows = pl.ds(256 * b, 256)
        unit, inverse = norm_parts(output[rows, :])
        fin = (unit * gain).astype(BF16)
        final[rows, :] = fin
        logits = jnp.concatenate([nn(fin, table[0]), nn(fin, table[1])], 1)
        top = jnp.max(logits, -1, keepdims=True)
        expo = jnp.exp(logits - top)
        total = jnp.sum(expo, -1, keepdims=True)
        picks = lax.broadcasted_iota(jnp.int32, logits.shape, 1) == targets[rows, :]
        picked = jnp.sum(jnp.where(picks, logits, 0.0), -1, keepdims=True)
        spot = segment * SEG + 256 * b + lax.broadcasted_iota(jnp.int32, (256, 1), 0)
        weight = jnp.where(spot < length, 1.0 / size, 0.0)
        terms = terms + jnp.sum((top + jnp.log(total) - picked) * weight, keepdims=True)
        grad = (expo * (1.0 / total) - jnp.where(picks, 1.0, 0.0)) * (weight * (1.0 / streams))
        grad_b = grad.astype(BF16)
        grad_logits[rows, :] = grad_b
        grad_final = nt(grad_b[:, 0:512], table[0]) + nt(grad_b[:, 512:1024], table[1])
        grad_here, gain_here = norm_back(unit, inverse, gain, grad_final)
        grad_out[rows, :] = grad_here
        gains = gains + gain_here
    for u in range(2):
        staged[u] = tn(final[...], grad_logits[:, 512 * u : 512 * (u + 1)]).astype(BF16)
    units = [(staged.at[u], 16 * u) for u in range(2)]
    copies(bits, place, half, (keep,), units, 16, sem, True)
    copies(bits, place, 1 - half, (send,), units, 16, sem, True)
    grad_gain[...] = jnp.broadcast_to(gains, grad_gain.shape)
    loss[...] = jnp.broadcast_to(terms, loss.shape)
    pltpu.make_async_copy(staged, staged, sem).wait()


VMEM = pl.BlockSpec(memory_space=pltpu.VMEM)
ANY = pl.BlockSpec(memory_space=pl.ANY)
SMEM = pl.BlockSpec(memory_space=pltpu.SMEM)


def shape(*dims, dtype=F32):
    return jax.ShapeDtypeStruct(dims, dtype)


def call(body, name, ins, outs, out_specs, scratch, flops):
    return pl.pallas_call(
        body,
        name=name,
        in_specs=ins,
        out_shape=outs,
        out_specs=out_specs,
        scratch_shapes=scratch,
        compiler_params=pltpu.CompilerParams(vmem_limit_bytes=VMEM_LIMIT),
        cost_estimate=pl.CostEstimate(flops=flops, bytes_accessed=1 << 23, transcendentals=0),
    )


SAVED = (
    shape(ROWS, D),
    shape(ROWS, D, dtype=BF16),
    shape(SEG, D, dtype=BF16),
    shape(SEG, D, dtype=BF16),
    shape(ROWS, D, dtype=BF16),
    shape(ROWS, D, dtype=BF16),
    shape(ROWS, D, dtype=BF16),
    shape(PAIRS, 2 * BLOCK, WIDE, dtype=BF16),
    shape(SEG, D, dtype=BF16),
    shape(5, D, D, dtype=BF16),
)


def run_attn_forward_first(bits, scalars, frames, pieces, table):
    outs = (shape(SEG, D),) + SAVED + (shape(16, D),)
    result = call(
        functools.partial(attn_forward, bits, 0),
        "attn_forward_first",
        [SMEM, VMEM, ANY, ANY, ANY, ANY, VMEM],
        outs,
        [VMEM] * len(outs),
        [pltpu.SemaphoreType.DMA, pltpu.VMEM((D, BLOCK), BF16), pltpu.SemaphoreType.DMA],
        5_000_000_000,
    )(scalars, frames, *pieces, table)
    return result[0], result[1:11], result[11]


def run_attn_forward(bits, scalars, memory, hidden, vecs, pieces, table):
    outs = (shape(SEG, D),) + SAVED
    result = call(
        functools.partial(attn_forward, bits, 4),
        "attn_forward",
        [SMEM, VMEM, VMEM, VMEM, ANY, ANY, ANY, ANY, VMEM],
        outs,
        [VMEM] * len(outs),
        [pltpu.SemaphoreType.DMA],
        5_000_000_000,
    )(scalars, memory, hidden, vecs, *pieces, table)
    return result[0], result[1:11]


ATTN_SCRATCH = [
    pltpu.VMEM((2 * BLOCK, 2 * BLOCK), BF16),
    pltpu.VMEM((SEG, D), BF16),
    pltpu.VMEM((D, ROWS), F32),
    pltpu.VMEM((D, ROWS), F32),
    pltpu.VMEM((D, ROWS), F32),
    pltpu.VMEM((SEG, D), F32),
    pltpu.VMEM((SEG, D), F32),
    pltpu.VMEM((5, D, D), BF16),
    pltpu.VMEM((BLOCK, D), F32),
    pltpu.SemaphoreType.DMA,
]


def run_attn_backward(bits, scalars, grad_mixed, saved, vecs, table):
    return call(
        functools.partial(attn_backward, bits, 4),
        "attn_backward",
        [SMEM] + [VMEM] * 13,
        (shape(GROUPS, 80, D, dtype=BF16), shape(GROUPS, 80, D, dtype=BF16), shape(SEG, D), shape(8, D)),
        [ANY, ANY, VMEM, VMEM],
        ATTN_SCRATCH,
        10_000_000_000,
    )(scalars, grad_mixed, *saved, vecs, table)


def run_attn_backward_last(bits, scalars, grad_mixed, saved, vecs, table, frames, *small_grads):
    return call(
        functools.partial(attn_backward, bits, 0),
        "attn_backward_last",
        [SMEM] + [VMEM] * 18,
        (shape(GROUPS, 96, D, dtype=BF16), shape(GROUPS, 96, D, dtype=BF16)),
        [ANY, ANY],
        ATTN_SCRATCH + [pltpu.VMEM((D, D), BF16), pltpu.SemaphoreType.DMA],
        10_000_000_000,
    )(scalars, grad_mixed, *saved, vecs, table, frames, *small_grads)


def run_feed_forward(bits, base, scalars, mixed, vecs, pieces):
    outs = (
        shape(SEG, D),
        shape(SEG, D, dtype=BF16),
        shape(SEG, FF, dtype=BF16),
        shape(SEG, FF, dtype=BF16),
        shape(4, D, D, dtype=BF16),
        shape(FF, D, dtype=BF16),
    )
    result = call(
        functools.partial(feed_forward, bits, base),
        "feed_forward",
        [SMEM, VMEM, VMEM, ANY, ANY, ANY, ANY],
        outs,
        [VMEM] * len(outs),
        [pltpu.SemaphoreType.DMA((2,))],
        4_000_000_000,
    )(scalars, mixed, vecs, *pieces)
    return result[0], result[1:]


def run_feed_backward(bits, base, scalars, grad_out, mixed, vecs, saved):
    return call(
        functools.partial(feed_backward, bits, base),
        "feed_backward",
        [SMEM] + [VMEM] * 8,
        (shape(GROUPS, 128, D, dtype=BF16), shape(GROUPS, 128, D, dtype=BF16), shape(SEG, D), shape(8, D)),
        [ANY, ANY, VMEM, VMEM],
        [
            pltpu.VMEM((SEG, FF), BF16),
            pltpu.VMEM((4, D, D), BF16),
            pltpu.VMEM((FF, D), BF16),
            pltpu.SemaphoreType.DMA((2,)),
        ],
        8_000_000_000,
    )(scalars, grad_out, mixed, vecs, *saved)


def run_head(bits, streams, scalars, output, targets, vecs, pieces):
    return call(
        functools.partial(head_pass, bits, streams),
        "head",
        [SMEM, VMEM, VMEM, VMEM, ANY, ANY, ANY, ANY],
        (
            shape(GROUPS, 32, D, dtype=BF16),
            shape(GROUPS, 32, D, dtype=BF16),
            shape(SEG, D),
            shape(8, D),
            shape(8, 128),
        ),
        [ANY, ANY, VMEM, VMEM, VMEM],
        [
            pltpu.VMEM((2, D, D), BF16),
            pltpu.VMEM((SEG, D), BF16),
            pltpu.VMEM((SEG, CODES), BF16),
            pltpu.VMEM((2, D, D), BF16),
            pltpu.SemaphoreType.DMA,
        ],
        2_000_000_000,
    )(scalars, output, targets, vecs, *pieces)


def spread(value, bits):
    count = lax.axis_size("dp")
    pairs = [
        (half * count + i, half * count + (i ^ bit)) for half, bit in enumerate(bits) for i in range(count)
    ]
    return lax.ppermute(value, ("section", "dp"), pairs)


def swap(value):
    return lax.ppermute(value, "section", [(0, 1), (1, 0)])


def gather_pieces(mine, bits):
    low = mine[None]
    steps = list(zip(*bits))
    for pair in steps[:-1]:
        low = jnp.concatenate([low, spread(low, pair)], 0)
    high = spread(low, steps[-1])
    return (low, high, swap(low), swap(high))


def reduce_pieces(keep, send, bits):
    total = keep.astype(F32) + swap(send).astype(F32)
    for pair in reversed(list(zip(*bits))):
        count = total.shape[0] // 2
        total = total[:count] + spread(total[count:].astype(BF16), pair).astype(F32)
    return total[0]


def add_up(value, bits):
    value = value + swap(value)
    for low, unused in zip(*bits):
        value = value + spread(value, (low, low))
    return value


def lanes_of(block):
    return [block[:, D * u : D * (u + 1)] for u in range(block.shape[1] // D)]


def sinus_table():
    where_at = (ROWS - 1 - jnp.arange(ROWS, dtype=jnp.int32)).astype(F32)[:, None]
    freqs = jnp.exp(-jnp.log(10000.0) * (2.0 * jnp.arange(D // 2, dtype=jnp.int32).astype(F32) / D))
    angles = where_at * freqs[None, :]
    return jnp.concatenate([jnp.sin(angles), jnp.cos(angles)], 1).astype(BF16)


def small_rows(w_in, vecs, gain, section):
    blank = jnp.zeros_like(vecs)
    return jnp.concatenate(
        [
            w_in,
            jnp.where(section == 0, vecs, blank),
            jnp.where(section == 0, blank, vecs),
            gain[None],
            jnp.zeros((BLOCK - 89, gain.shape[0]), vecs.dtype),
        ],
        0,
    )


def pack_shards(section, w_attn, w_out, w_pos, w_up, w_down, layer_vecs, w_in, w_head, gain_final):
    attn = lanes_of(w_attn[0]) + [w_out[0], w_pos[0]]
    ups = lanes_of(w_up[0])
    heads = lanes_of(w_head)
    small = small_rows(w_in, layer_vecs[0], gain_final, section)
    mark = lax.broadcasted_iota(jnp.int32, small.shape, 0)
    vecs_only = jnp.where((mark >= FEATS) & (mark < FEATS + 8), small, 0.0)
    small, vecs_only = (
        jnp.pad(jnp.transpose(item), ((0, 0), (0, D - BLOCK))) for item in (small, vecs_only)
    )

    def half_of(half, tail):
        rows = slice(16 * half, 16 * half + 16)
        return jnp.concatenate(
            [item[rows] for item in attn]
            + [item[rows] for item in ups]
            + [w_down[0, 64 * half : 64 * half + 64], tail[rows]],
            0,
        ).astype(BF16)

    first = section == 0
    kept = jnp.where(first, half_of(0, small), half_of(1, small))
    got = swap(jnp.where(first, half_of(1, vecs_only), half_of(0, vecs_only)))
    zero = jnp.where(first, kept, got)
    one = jnp.where(first, got, kept)
    head = jnp.where(
        first,
        jnp.concatenate([item[:16] for item in heads], 0),
        jnp.concatenate([item[16:] for item in heads], 0),
    ).astype(BF16)
    return (
        jnp.concatenate([zero[:80], kept[208:] + got[208:]], 0),
        zero[80:208],
        one[:80],
        jnp.concatenate([one[80:208], head], 0),
    )


def halves(whole, rows):
    return whole.reshape(GROUPS, 2, rows, whole.shape[1]).transpose(1, 0, 2, 3)


def gather_whole(section, w_attn, w_out, w_pos, w_up, w_down, layer_vecs, w_in, w_head, gain_final):
    def over(value, axis):
        return lax.all_gather(value.astype(BF16), "dp", axis=axis, tiled=True)

    def layers(value):
        return lax.all_gather(over(value[0], 0), "section", axis=0)

    attn, out, pos, up, down = (layers(item) for item in (w_attn, w_out, w_pos, w_up, w_down))
    vecs = lax.all_gather(over(layer_vecs[0], 1), "section", axis=0)
    small = jnp.concatenate(
        [over(w_in, 1), vecs[0], vecs[1], over(gain_final, 0)[None], jnp.zeros((BLOCK - 89, D), BF16)], 0
    )
    small = jnp.pad(jnp.transpose(small), ((0, 0), (0, D - BLOCK)))
    head = over(w_head, 0)

    def pieces(units):
        both = jnp.concatenate([halves(item, item.shape[0] // 32) for item in units], 2)
        own = lax.dynamic_index_in_dim(both, section, 0, keepdims=False)
        other = lax.dynamic_index_in_dim(both, 1 - section, 0, keepdims=False)
        return (own[:8], own[8:], other[:8], other[8:])

    return (
        pieces(lanes_of(attn[0]) + [out[0], pos[0], small]),
        pieces(lanes_of(up[0]) + [down[0]]),
        pieces(lanes_of(attn[1]) + [out[1], pos[1]]),
        pieces(lanes_of(up[1]) + [down[1]] + lanes_of(head)),
    )


def own_grads(section, attn_zero, feed_zero, attn_one, feed_one, head):
    first = section == 0
    zero = jnp.concatenate([attn_zero[:80], feed_zero], 0)
    one = jnp.concatenate([attn_one, feed_one], 0)
    both = jnp.concatenate([head, attn_zero[80:96]], 0)
    kept = jnp.concatenate([jnp.where(first, zero, one), both], 0)
    got = swap(jnp.concatenate([jnp.where(first, one, zero), both], 0))
    low = jnp.where(first, kept, got)
    high = jnp.where(first, got, kept)

    def unit(start, rows):
        return jnp.concatenate([low[start : start + rows], high[start : start + rows]], 0)

    small = jnp.transpose(unit(240, 16)[:, :BLOCK])
    return (
        jnp.concatenate([unit(16 * u, 16) for u in range(3)], 1),
        unit(48, 16),
        unit(64, 16),
        jnp.concatenate([unit(80 + 16 * u, 16) for u in range(4)], 1),
        unit(144, 64),
        jnp.where(first, small[80:84], small[84:88]),
        small[:80],
        jnp.concatenate([unit(208 + 16 * u, 16) for u in range(2)], 1),
        small[88],
    )


def whole_grads(section, sums):
    count = lax.axis_size("dp")
    place = lax.axis_index("dp")
    both = [lax.all_gather(lax.psum(item, "dp"), "section", axis=0) for item in sums]

    def unit(index, start, rows):
        item = both[index][:, :, start : start + rows]
        return item.transpose(1, 0, 2, 3).reshape(GROUPS * 2 * rows, D)

    def layer(attn, feed):
        return (
            jnp.concatenate([unit(attn, 16 * u, 16) for u in range(3)], 1),
            unit(attn, 48, 16),
            unit(attn, 64, 16),
            jnp.concatenate([unit(feed, 16 * u, 16) for u in range(4)], 1),
            unit(feed, 64, 64),
        )

    small = jnp.transpose(unit(0, 80, 16)[:, :BLOCK])
    zero = layer(0, 1) + (small[80:84],)
    one = layer(2, 3) + (small[84:88],)
    ends = (small[:80], jnp.concatenate([unit(4, 16 * u, 16) for u in range(2)], 1), small[88])
    squares = sum((jnp.sum(item * item) for item in zero + one + ends))
    dims = (0, 0, 0, 0, 0, 1, 1, 0, 0)
    grads = tuple((jnp.where(section == 0, a, b) for a, b in zip(zero, one))) + ends
    return squares, tuple(
        (
            lax.dynamic_slice_in_dim(item, place * (item.shape[dim] // count), item.shape[dim] // count, dim)
            for item, dim in zip(grads, dims)
        )
    )


def adam_step(weight, grad, first, second, rate, decay, factor):
    grad = grad * factor
    first = 0.9 * first + 0.1 * grad
    second = 0.999 * second + 0.001 * grad * grad
    ratio = first / (1.0 - 0.9**STEP) / (jnp.sqrt(second / (1.0 - 0.999**STEP)) + 1e-08)
    return (weight - rate * (ratio + decay * weight), first, second)


def local(frames, targets, lengths, *state):
    params, firsts, seconds = (state[:9], state[9:18], state[18:])
    section = lax.axis_index("section")
    streams = lax.axis_size("dp")
    ringed = streams == GROUPS
    if ringed:
        bits = ((4, 8, 1, 2), (4, 8, 2, 1))
        place = lax.axis_index("dp")
        chunks = [gather_pieces(item, bits) for item in pack_shards(section, *params)]
    else:
        bits = ((1, 2, 4, 8), (1, 2, 4, 8))
        place = jnp.int32(0)
        chunks = gather_whole(section, *params)
    length = lengths[0]
    scalars = jnp.stack([place, section, length, section]).astype(jnp.int32)
    table = sinus_table()
    rows = lax.dynamic_slice_in_dim(
        jnp.pad(frames[0], ((MEM, 0), (0, BLOCK - FEATS))), section * SEG, ROWS, 0
    )
    codes = lax.dynamic_slice_in_dim(targets[0], section * SEG, SEG, 0)[:, None]

    mixed_zero, saved_zero, vecs = run_attn_forward_first(bits, scalars, rows, chunks[0], table)
    out_zero, fed_zero = run_feed_forward(bits, 0, scalars, mixed_zero, vecs, chunks[1])
    memory = lax.ppermute(out_zero[SEG - MEM :], "section", [(0, 1)])
    mixed_one, saved_one = run_attn_forward(bits, scalars, memory, out_zero, vecs, chunks[2], table)
    out_one, fed_one = run_feed_forward(bits, 4, scalars, mixed_one, vecs, chunks[3])
    head_keep, head_send, grad, gain_final, loss = run_head(
        bits, streams, scalars, out_one, codes, vecs, chunks[3]
    )
    feed_keep, feed_send, grad, gain_one = run_feed_backward(bits, 4, scalars, grad, mixed_one, vecs, fed_one)
    attn_keep, attn_send, grad, vecs_one = run_attn_backward(bits, scalars, grad, saved_one, vecs, table)
    feed_keep_zero, feed_send_zero, grad, gain_zero = run_feed_backward(
        bits, 0, scalars, grad, mixed_zero, vecs, fed_zero
    )
    attn_keep_zero, attn_send_zero = run_attn_backward_last(
        bits, scalars, grad, saved_zero, vecs, table, rows, gain_zero, vecs_one, gain_one, gain_final
    )
    pairs = (
        (attn_keep_zero, attn_send_zero),
        (feed_keep_zero, feed_send_zero),
        (attn_keep, attn_send),
        (feed_keep, feed_send),
        (head_keep, head_send),
    )
    if ringed:
        sums = [reduce_pieces(keep, send, bits) for keep, send in pairs]
        grads = own_grads(section, *sums)
        squares = sum((jnp.sum(item * item) for item in sums))
        total = add_up(jnp.stack([squares, loss[0, 0]])[None], bits)
        squares, loss_sum = total[0, 0], total[0, 1]
    else:
        sums = [keep.astype(F32) + swap(send).astype(F32) for keep, send in pairs]
        squares, grads = whole_grads(section, sums)
        loss_sum = lax.psum(loss[0, 0], ("section", "dp"))
    grad_norm = jnp.sqrt(squares)
    factor = jnp.minimum(1.0, CLIP / (grad_norm + 1e-06))
    results = []
    for index in range(9):
        vector = index in (5, 8)
        grad = grads[index][None] if index < 6 else grads[index]
        results.append(
            adam_step(
                params[index],
                grad,
                firsts[index],
                seconds[index],
                0.3 if vector else 0.03,
                0.0 if vector else 0.01,
                factor,
            )
        )
    news, moms, sqs = zip(*results)
    return (*news, *moms, *sqs, grad_norm, loss_sum)


def solution(mesh):
    weights = (
        P("section", "dp", None),
        P("section", "dp", None),
        P("section", "dp", None),
        P("section", "dp", None),
        P("section", "dp", None),
        P("section", None, "dp"),
        P(None, "dp"),
        P("dp", None),
        P("dp"),
    )
    return jax.shard_map(
        local,
        mesh=mesh,
        in_specs=(P("dp", None, None), P("dp", None), P("dp")) + weights * 3,
        out_specs=weights * 3 + (P(), P()),
        check_vma=False,
    )
```

time: 2110 us -> 388 us (0.18)
  local copies, waits for them, and re-layouts: 630 us -> 22.7 us
  waiting for transfers between devices: 725 us -> 119 us
  blocking collectives: 329 us -> 0 us
  matrix products: 243 us -> 0 us
  Pallas kernels: 0 us -> 144 us
  other arithmetic: 121 us -> 25.8 us
  starting transfers between devices: 7.47 us -> 63.4 us
    psum x2 -> x0, waiting for transfers between devices: 365 us -> none  [the longest x1 364 us: local(): lax.psum((layer_grads[0], layer_grads[1], layer_grads[2], layer_grads[3],...]
    ppermute x4 -> x57, waiting for transfers between devices: 341 us -> 119 us  [the longest x40 117 us: spread(): return lax.ppermute(value, ('section', 'dp'), pairs)]
    dot_general x152 -> x0, matrix products: 210 us -> none  [the longest x104 102 us: einmul(): return jnp.einsum(form, left, right, preferred_element_type=jnp.float32)]
    reshape x32 -> x0, local copies, waits for them, and re-layouts: 185 us -> none  [the longest x24 154 us: skew(): jnp.pad(block, ((0, 0), (0, 0), (0, 1))).reshape(count, rows * (cols + 1))]
    all_gather x4 -> x0, blocking collectives: 168 us -> none  [the longest x1 44.8 us: local(): lax.all_gather(w_pos[0].astype(jnp.bfloat16), 'dp', axis=0, tiled=True)]
    dynamic_slice x155 -> x1, local copies, waits for them, and re-layouts: 151 us -> 0.81 us  [local(): lax.dynamic_slice_in_dim(jnp.pad(frames[0], ((MEM, 0), (0, BLOCK - FEATS)...]
    pallas_call x0 -> x9, Pallas kernels: none -> 144 us  [the longest x1 26.4 us: run_attn_backward_last(): call(functools.partial(attn_backward, bits, 0), 'attn_backward_last', [SM...]
    psum x3 -> x0, blocking collectives: 121 us -> none  [the longest x1 76.1 us: local(): lax.psum((layer_grads[0], layer_grads[1], layer_grads[2], layer_grads[3],...]
  transfers between devices with their start and end apart: 10 -> 57, of which waited for: 6 -> 28; matrix products, arithmetic and copies ran while one was open for 7% -> 6% of each run, Pallas kernels for 0% -> 33%
where the time goes in v1:
time: 388 us; the launch traced here: 383 us
  Pallas kernels  144 us (37%)
  waiting for transfers between devices  119 us (31%)
  starting transfers between devices  63.4 us (16%)
  other arithmetic  25.8 us (7%)
  local copies, waits for them, and re-layouts  22.7 us (6%)
  between operations  7.95 us (2%)
    ppermute x40, waiting for transfers between devices, spread(): return lax.ppermute(value, ('section', 'dp'), pairs)  117 us
    ppermute x40, starting transfers between devices, spread(): return lax.ppermute(value, ('section', 'dp'), pairs)  56.1 us
    pallas_call x1, Pallas kernels, run_attn_backward_last(): call(functools.partial(attn_backward, bits, 0), 'attn_backward_last', [SM...  26.4 us
    pallas_call x1, Pallas kernels, run_attn_backward(): call(functools.partial(attn_backward, bits, 4), 'attn_backward', [SMEM] +...  25.7 us
    pallas_call x2, Pallas kernels, run_feed_backward(): call(functools.partial(feed_backward, bits, base), 'feed_backward', [SMEM...  23.3 us
    pallas_call x1, Pallas kernels, run_attn_forward(): call(functools.partial(attn_forward, bits, 4), 'attn_forward', [SMEM, VME...  20.4 us
    pallas_call x1, Pallas kernels, run_attn_forward_first(): call(functools.partial(attn_forward, bits, 0), 'attn_forward_first', [SME...  20.4 us
    pallas_call x2, Pallas kernels, run_feed_forward(): call(functools.partial(feed_forward, bits, base), 'feed_forward', [SMEM,...  20.1 us
  transfers between devices with their start and end apart: 57, of which 28 were waited for; matrix products, arithmetic and copies ran while one was open for 6% of the time, Pallas kernels for 33%

profile of v1, /device:TPU:0, one launch (start us, length us, event | category | flops | bytes accessed | tf_op | source)
XLA Modules:
  0.0 382.9 jit_solution(5665044917238379888)
XLA Ops:
  16.9 3.0 collective-permute-start.1
  20.0 2.0 collective-permute-start.20
  22.0 1.5 collective-permute-done.1
  23.5 3.1 collective-permute-start.2
  26.6 3.9 %collective-permute-start.8 = (bf16[2,128,512]{2,1,0:T(8,128)(2,1)S(1)}, bf16[2,128,512]{2,1,0:T(8,128)(2,1)S(1)}, u32[]{:S(2)}, u32[]{:S(2)}) collective-permute-start(bf16[2,128,512]{2,1,0:T(8,128)(2,1)S(1)} %pad_maximum_fusion.16), channel_id=1, source_target_pairs={{0,8},{1,9},{2,10},{3,11},{4,12},{5,13},{6,14},{7,15},{8,0},{9,1},... | collective-permute-start | bytes 786440 | tf_op jit(solution)/shard_map/ppermute | solution.py:575
  30.5 4.2 %collective-permute-done.20 = bf16[1,160,512]{2,1,0:T(8,128)(2,1)S(1)} collective-permute-done((bf16[1,160,512]{2,1,0:T(8,128)(2,1)S(1)}, bf16[1,160,512]{2,1,0:T(8,128)(2,1)S(1)}, u32[]{:S(2)}, u32[]{:S(2)}) %collective-permute-start.20) | collective-permute-done | bytes 163872 | tf_op jit(solution)/shard_map/ppermute | solution.py:575
  34.8 14.0 %collective-permute-done.2 = bf16[2,96,512]{2,1,0:T(8,128)(2,1)S(1)} collective-permute-done((bf16[2,96,512]{2,1,0:T(8,128)(2,1)S(1)}, bf16[2,96,512]{2,1,0:T(8,128)(2,1)S(1)}, u32[]{:S(2)}, u32[]{:S(2)}) %collective-permute-start.2) | collective-permute-done | bytes 196640 | tf_op jit(solution)/shard_map/ppermute | solution.py:575
  48.8 2.1 collective-permute-start.3
  50.9 3.5 collective-permute-done.8
  54.4 2.1 collective-permute-start.9
  56.5 3.4 collective-permute-done.21
  60.0 1.7 collective-permute-start.22
  61.8 1.6 collective-permute-start.4
  63.4 1.5 collective-permute-done.9
  65.0 3.4 collective-permute-start.10
  68.4 1.2 collective-permute-start.14
  69.6 3.5 collective-permute-done.14
  73.1 2.3 collective-permute-start.15
  75.5 5.7 %collective-permute-done.15 = bf16[2,80,512]{2,1,0:T(8,128)(2,1)S(1)} collective-permute-done((bf16[2,80,512]{2,1,0:T(8,128)(2,1)S(1)}, bf16[2,80,512]{2,1,0:T(8,128)(2,1)S(1)}, u32[]{:S(2)}, u32[]{:S(2)}) %collective-permute-start.15) | collective-permute-done | bytes 163872 | tf_op jit(solution)/shard_map/ppermute | solution.py:575
  82.0 1.6 collective-permute-start.16
  84.9 1.1 copy.72
  86.8 6.2 %collective-permute-done.16 = bf16[4,80,512]{2,1,0:T(8,128)(2,1)} collective-permute-done((bf16[4,80,512]{2,1,0:T(8,128)(2,1)}, bf16[4,80,512]{2,1,0:T(8,128)(2,1)}, u32[]{:S(2)}, u32[]{:S(2)}) %collective-permute-start.16) | collective-permute-done | bytes 327712 | tf_op jit(solution)/shard_map/ppermute | solution.py:575
  92.9 1.2 collective-permute-start.12
  94.1 3.3 fusion
  97.4 2.0 pad_maximum_fusion.8.refs_4_
  99.4 2.0 collective-permute-start.17
  103.0 20.4 %attn_forward_first.1 = (f32[512,512]{1,0:T(8,128)}, f32[768,512]{1,0:T(8,128)}, bf16[768,512]{1,0:T(8,128)(2,1)}, bf16[512,512]{1,0:T(8,128)(2,1)}, bf16[512,51...) custom-call(s32[4]{0:T(128)} %pad_add_fusion.refs_0_.scalars, ...), custom_call_target="tpu_custom_call" | custom-call | flops 5000000000 | bytes 8388608 | tf_op jit(solution)/shard_map/attn_forward_first/pallas_call | solution.py:444
  125.5 10.0 %feed_forward.2 = (f32[512,512]{1,0:T(8,128)}, bf16[512,512]{1,0:T(8,128)(2,1)}, bf16[512,2048]{1,0:T(8,128)(2,1)}, bf16[512,2048]{1,0:T(8,128)(2,1)}, bf16[4,51...) custom-call(s32[4]{0:T(128)} %pad_add_fusion.refs_0_.scalars, f32[512,512]{1,0:T(8,128)} %get-tuple-element.83.mixed, ...), custom_call_target="tpu_custom_call" | custom-call | flops 4000000000 | bytes 8388608 | tf_op jit(solution)/shard_map/feed_forward/pallas_call | solution.py:517
  136.6 2.9 collective-permute-start.13
  140.3 20.4 %attn_forward.1 = (f32[512,512]{1,0:T(8,128)}, f32[768,512]{1,0:T(8,128)}, bf16[768,512]{1,0:T(8,128)(2,1)}, bf16[512,512]{1,0:T(8,128)(2,1)}, bf16[512,512]{1,0...) custom-call(s32[4]{0:T(128)} %pad_add_fusion.refs_0_.scalars, ...), custom_call_target="tpu_custom_call" | custom-call | flops 5000000000 | bytes 8388608 | tf_op jit(solution)/shard_map/attn_forward/pallas_call | solution.py:458
  160.8 1.1 copy-done.42
  161.9 10.0 %feed_forward.3 = (f32[512,512]{1,0:T(8,128)}, bf16[512,512]{1,0:T(8,128)(2,1)}, bf16[512,2048]{1,0:T(8,128)(2,1)}, bf16[512,2048]{1,0:T(8,128)(2,1)}, bf16[4,51...) custom-call(s32[4]{0:T(128)} %pad_add_fusion.refs_0_.scalars, f32[512,512]{1,0:T(8,128)} %get-tuple-element.86.mixed, ...), custom_call_target="tpu_custom_call" | custom-call | flops 4000000000 | bytes 8388608 | tf_op jit(solution)/shard_map/feed_forward/pallas_call | solution.py:517
  171.9 8.1 %head.1 = (bf16[16,32,512]{2,1,0:T(8,128)(2,1)}, bf16[16,32,512]{2,1,0:T(8,128)(2,1)}, f32[512,512]{1,0:T(8,128)}, f32[8,512]{1,0:T(8,128)}, f32[8,128]{1,0:T(8,128)}) custom-call(s32[4]{0:T(128)} %pad_add_fusion.refs_0_.scalars, f32[512,512]{1,0:T(8,128)} %get-tuple-element.87.output, s32[512,1]{1,0:T(8,128)} %copy.76.targets, ...), custom_call_target="tpu_custom_call" | custom-call | flops 2000000000 | bytes 8388608 | tf_op jit(solution)/shard_map/head/pallas_call | solution.py:547
  180.4 11.6 %feed_backward.2 = (bf16[16,128,512]{2,1,0:T(8,128)(2,1)}, bf16[16,128,512]{2,1,0:T(8,128)(2,1)}, f32[512,512]{1,0:T(8,128)}, f32[8,512]{1,0:T(8,128)}) custom-call(s32[4]{0:T(128)} %pad_add_fusion.refs_0_.scalars, f32[512,512]{1,0:T(8,128)} %get-tuple-element.88.grad_out, f32[512,512]{1,0:T(8,128)} %get-tuple-element.86.mixed, ...), custom_call_target="tpu_custom_call" | custom-call | flops 8000000000 | bytes 8388608 | tf_op jit(solution)/shard_map/feed_backward/pallas_call | solution.py:530
  192.0 25.7 %attn_backward.1 = (bf16[16,80,512]{2,1,0:T(8,128)(2,1)}, bf16[16,80,512]{2,1,0:T(8,128)(2,1)}, f32[512,512]{1,0:T(8,128)}, f32[8,512]{1,0:T(8,128)}) custom-call(s32[4]{0:T(128)} %pad_add_fusion.refs_0_.scalars, f32[512,512]{1,0:T(8,128)} %get-tuple-element.94.refs_1_, f32[768,512]{1,0:T(8,128)} %get-tuple-element.95.refs_2_, ...), custom_call_target="tpu_custom_call" | custom-call | flops 10000000000 | bytes 8388608 | tf_op jit(solution)/shard_map/attn_backward/pallas_call | solution.py:485
  218.1 11.7 %feed_backward.3 = (bf16[16,128,512]{2,1,0:T(8,128)(2,1)}, bf16[16,128,512]{2,1,0:T(8,128)(2,1)}, f32[512,512]{1,0:T(8,128)}, f32[8,512]{1,0:T(8,128)}) custom-call(s32[4]{0:T(128)} %pad_add_fusion.refs_0_.scalars, f32[512,512]{1,0:T(8,128)} %get-tuple-element.105.grad_out, f32[512,512]{1,0:T(8,128)} %get-tuple-element.83.mixed, ...), custom_call_target="tpu_custom_call" | custom-call | flops 8000000000 | bytes 8388608 | tf_op jit(solution)/shard_map/feed_backward/pallas_call | solution.py:530
  230.0 1.2 collective-permute-start.47
  231.2 26.4 %attn_backward_last.1 = (bf16[16,96,512]{2,1,0:T(8,128)(2,1)}, bf16[16,96,512]{2,1,0:T(8,128)(2,1)}) custom-call(s32[4]{0:T(128)} %pad_add_fusion.refs_0_.scalars, f32[512,512]{1,0:T(8,128)} %get-tuple-element.111.refs_1_, f32[768,512]{1,0:T(8,128)} %get-tuple-element.112.refs_2_, bf16[768,512]{1,0:T(8,128)(2,1)} %get-tuple-element.113.refs_3_, ...), custom_call_target="tpu_custom_call" | custom-call | flops 10000000000 | bytes 8388608 | tf_op jit(solution)/shard_map/attn_backward_last/pallas_call | solution.py:497
  259.2 4.1 %collective-permute-done.48 = bf16[4,32,512]{2,1,0:T(8,128)(2,1)S(1)} collective-permute-done((bf16[4,32,512]{2,1,0:T(8,128)(2,1)S(1)}, bf16[4,32,512]{2,1,0:T(8,128)(2,1)S(1)}, u32[]{:S(2)}, u32[]{:S(2)}) %collective-permute-start.48) | collective-permute-done | bytes 131104 | tf_op jit(solution)/shard_map/ppermute | solution.py:575
  264.9 4.6 %collective-permute-done.49 = bf16[2,32,512]{2,1,0:T(8,128)(2,1)S(1)} collective-permute-done((bf16[2,32,512]{2,1,0:T(8,128)(2,1)S(1)}, bf16[2,32,512]{2,1,0:T(8,128)(2,1)S(1)}, u32[]{:S(2)}, u32[]{:S(2)}) %collective-permute-start.49) | collective-permute-done | bytes 65568 | tf_op jit(solution)/shard_map/ppermute | solution.py:575
  270.1 1.2 slice.511
  271.3 2.3 collective-permute-done.50
  275.1 1.5 collective-permute-start.38
  278.2 7.6 %collective-permute-done.38 = bf16[4,80,512]{2,1,0:T(8,128)(2,1)S(1)} collective-permute-done((bf16[4,80,512]{2,1,0:T(8,128)(2,1)S(1)}, bf16[4,80,512]{2,1,0:T(8,128)(2,1)S(1)}, u32[]{:S(2)}, u32[]{:S(2)}) %collective-permute-start.38) | collective-permute-done | bytes 327712 | tf_op jit(solution)/shard_map/ppermute | solution.py:575
  286.0 2.7 collective-permute-start.39
  290.9 1.5 collective-permute-start.42
  292.4 1.5 collective-permute-done.39
  294.0 3.2 collective-permute-start.40
  297.2 4.0 %collective-permute-done.28 = bf16[4,96,512]{2,1,0:T(8,128)(2,1)S(1)} collective-permute-done((bf16[4,96,512]{2,1,0:T(8,128)(2,1)S(1)}, bf16[4,96,512]{2,1,0:T(8,128)(2,1)S(1)}, u32[]{:S(2)}, u32[]{:S(2)}) %collective-permute-start.28) | collective-permute-done | bytes 393248 | tf_op jit(solution)/shard_map/ppermute | solution.py:575
  301.3 2.1 collective-permute-start.29
  304.1 6.0 %collective-permute-done.29 = bf16[2,96,512]{2,1,0:T(8,128)(2,1)S(1)} collective-permute-done((bf16[2,96,512]{2,1,0:T(8,128)(2,1)S(1)}, bf16[2,96,512]{2,1,0:T(8,128)(2,1)S(1)}, u32[]{:S(2)}, u32[]{:S(2)}) %collective-permute-start.29) | collective-permute-done | bytes 196640 | tf_op jit(solution)/shard_map/ppermute | solution.py:575
  310.9 1.2 collective-permute-start.33
  312.0 8.4 %collective-permute-done.42 = bf16[8,128,512]{2,1,0:T(8,128)(2,1)S(1)} collective-permute-done((bf16[8,128,512]{2,1,0:T(8,128)(2,1)S(1)}, bf16[8,128,512]{2,1,0:T(8,128)(2,1)S(1)}, u32[]{:S(2)}, u32[]{:S(2)}) %collective-permute-start.42) | collective-permute-done | bytes 1048608 | tf_op jit(solution)/shard_map/ppermute | solution.py:575
  322.7 2.2 collective-permute-start.34
  324.9 5.1 %collective-permute-done.43 = bf16[4,128,512]{2,1,0:T(8,128)(2,1)S(1)} collective-permute-done((bf16[4,128,512]{2,1,0:T(8,128)(2,1)S(1)}, bf16[4,128,512]{2,1,0:T(8,128)(2,1)S(1)}, u32[]{:S(2)}, u32[]{:S(2)}) %collective-permute-start.43) | collective-permute-done | bytes 524320 | tf_op jit(solution)/shard_map/ppermute | solution.py:575
  330.3 2.2 collective-permute-start.44
  332.5 9.6 %collective-permute-done.34 = bf16[2,128,512]{2,1,0:T(8,128)(2,1)S(1)} collective-permute-done((bf16[2,128,512]{2,1,0:T(8,128)(2,1)S(1)}, bf16[2,128,512]{2,1,0:T(8,128)(2,1)S(1)}, u32[]{:S(2)}, u32[]{:S(2)}) %collective-permute-start.34) | collective-permute-done | bytes 262176 | tf_op jit(solution)/shard_map/ppermute | solution.py:575
  342.2 4.6 %collective-permute-done.44 = bf16[2,128,512]{2,1,0:T(8,128)(2,1)S(1)} collective-permute-done((bf16[2,128,512]{2,1,0:T(8,128)(2,1)S(1)}, bf16[2,128,512]{2,1,0:T(8,128)(2,1)S(1)}, u32[]{:S(2)}, u32[]{:S(2)}) %collective-permute-start.44) | collective-permute-done | bytes 262176 | tf_op jit(solution)/shard_map/ppermute | solution.py:575
  347.1 2.6 collective-permute-done.35
  356.9 3.5 collective-permute-done.53
  361.2 1.4 collective-permute-start.54
  362.6 3.1 collective-permute-done.54
  365.8 3.3 collective-permute-done.55
  369.4 3.3 collective-permute-done.56
  (290 shorter events, 51.7 us)
Async XLA Ops:
  0.7 138.8 %copy-start = (s32[1,1024]{1,0:T(1,128)S(1)}, s32[1,1024]{1,0:T(1,128)}, u32[]{:S(2)}) copy-start(s32[1,1024]{1,0:T(1,128)} %param.31) | copy-start | bytes 12292
  0.7 14.9 %copy-start.15 = (f32[32,1024]{1,0:T(8,128)S(1)}, f32[32,1024]{1,0:T(8,128)}, u32[]{:S(2)}) copy-start(f32[32,1024]{1,0:T(8,128)} %param.40) | copy-start | bytes 393220
  15.1 1.6 collective-permute-start
  16.9 6.6 %collective-permute-start.1 = (bf16[1,96,512]{2,1,0:T(8,128)(2,1)S(1)}, bf16[1,96,512]{2,1,0:T(8,128)(2,1)S(1)}, u32[]{:S(2)}, u32[]{:S(2)}) collective-permute-start(bf16[1,96,512]{2,1,0:T(8,128)(2,1)S(1)} %maximum_bitcast_fusion.1), channel_id=1, source_target_pairs={{0,4},{1,5},{2,6},{3,7},{4,0},{5,1},{6,2},{7,3},{8,12},{9,13},{10,... | collective-permute-start | bytes 294920 | tf_op jit(solution)/shard_map/ppermute | solution.py:575
  19.9 6.7 %collective-permute-start.7 = (bf16[1,128,512]{2,1,0:T(8,128)(2,1)S(1)}, bf16[1,128,512]{2,1,0:T(8,128)(2,1)S(1)}, u32[]{:S(2)}, u32[]{:S(2)}) collective-permute-start(bf16[1,128,512]{2,1,0:T(8,128)(2,1)S(1)} %slice_bitcast_fusion.3), channel_id=1, source_target_pairs={{0,4},{1,5},{2,6},{3,7},{4,0},{5,1},{6,2},{7,3},{8,12},{9,13},{10,... | collective-permute-start | bytes 393224 | tf_op jit(solution)/shard_map/ppermute | solution.py:575
  20.0 14.7 %collective-permute-start.20 = (bf16[1,160,512]{2,1,0:T(8,128)(2,1)S(1)}, bf16[1,160,512]{2,1,0:T(8,128)(2,1)S(1)}, u32[]{:S(2)}, u32[]{:S(2)}) collective-permute-start(bf16[1,160,512]{2,1,0:T(8,128)(2,1)S(1)} %maximum_bitcast_fusion), channel_id=1, source_target_pairs={{0,4},{1,5},{2,6},{3,7},{4,0},{5,1},{6,2},{7,3},{8,12},{9,13},{10,... | collective-permute-start | bytes 491528 | tf_op jit(solution)/shard_map/ppermute | solution.py:575
  23.5 25.3 %collective-permute-start.2 = (bf16[2,96,512]{2,1,0:T(8,128)(2,1)S(1)}, bf16[2,96,512]{2,1,0:T(8,128)(2,1)S(1)}, u32[]{:S(2)}, u32[]{:S(2)}) collective-permute-start(bf16[2,96,512]{2,1,0:T(8,128)(2,1)S(1)} %pad_maximum_fusion.17), channel_id=1, source_target_pairs={{0,8},{1,9},{2,10},{3,11},{4,12},{5,13},{6,14},{7,15},{8,0},{9,1},... | collective-permute-start | bytes 589832 | tf_op jit(solution)/shard_map/ppermute | solution.py:575
  26.6 27.7 %collective-permute-start.8 = (bf16[2,128,512]{2,1,0:T(8,128)(2,1)S(1)}, bf16[2,128,512]{2,1,0:T(8,128)(2,1)S(1)}, u32[]{:S(2)}, u32[]{:S(2)}) collective-permute-start(bf16[2,128,512]{2,1,0:T(8,128)(2,1)S(1)} %pad_maximum_fusion.16), channel_id=1, source_target_pairs={{0,8},{1,9},{2,10},{3,11},{4,12},{5,13},{6,14},{7,15},{8,0},{9,1},... | collective-permute-start | bytes 786440 | tf_op jit(solution)/shard_map/ppermute | solution.py:575
  34.7 25.2 %collective-permute-start.21 = (bf16[2,160,512]{2,1,0:T(8,128)(2,1)S(1)}, bf16[2,160,512]{2,1,0:T(8,128)(2,1)S(1)}, u32[]{:S(2)}, u32[]{:S(2)}) collective-permute-start(bf16[2,160,512]{2,1,0:T(8,128)(2,1)S(1)} %pad_maximum_fusion.15), channel_id=1, source_target_pairs={{0,8},{1,9},{2,10},{3,11},{4,12},{5,13},{6,14},{7,15},{8,0},{9,1},... | collective-permute-start | bytes 983048 | tf_op jit(solution)/shard_map/ppermute | solution.py:575
  48.8 12.9 %collective-permute-start.3 = (bf16[4,96,512]{2,1,0:T(8,128)(2,1)S(1)}, bf16[4,96,512]{2,1,0:T(8,128)(2,1)S(1)}, u32[]{:S(2)}, u32[]{:S(2)}) collective-permute-start(bf16[4,96,512]{2,1,0:T(8,128)(2,1)S(1)} %pad_maximum_fusion.13), channel_id=1, source_target_pairs={{0,1},{1,0},{2,3},{3,2},{4,5},{5,4},{6,7},{7,6},{8,9},{9,8},{10,11... | collective-permute-start | bytes 1179656 | tf_op jit(solution)/shard_map/ppermute | solution.py:575
  54.4 10.4 %collective-permute-start.9 = (bf16[4,128,512]{2,1,0:T(8,128)(2,1)S(1)}, bf16[4,128,512]{2,1,0:T(8,128)(2,1)S(1)}, u32[]{:S(2)}, u32[]{:S(2)}) collective-permute-start(bf16[4,128,512]{2,1,0:T(8,128)(2,1)S(1)} %pad_maximum_fusion.10), channel_id=1, source_target_pairs={{0,1},{1,0},{2,3},{3,2},{4,5},{5,4},{6,7},{7,6},{8,9},{9,8},{10,11... | collective-permute-start | bytes 1572872 | tf_op jit(solution)/shard_map/ppermute | solution.py:575
  60.0 23.6 %collective-permute-start.22 = (bf16[4,160,512]{2,1,0:T(8,128)(2,1)S(1)}, bf16[4,160,512]{2,1,0:T(8,128)(2,1)S(1)}, u32[]{:S(2)}, u32[]{:S(2)}) collective-permute-start(bf16[4,160,512]{2,1,0:T(8,128)(2,1)S(1)} %pad_maximum_fusion.9), channel_id=1, source_target_pairs={{0,1},{1,0},{2,3},{3,2},{4,5},{5,4},{6,7},{7,6},{8,9},{9,8},{10,11... | collective-permute-start | bytes 1966088 | tf_op jit(solution)/shard_map/ppermute | solution.py:575
  61.8 21.9 %copy-start.8 = (bf16[8,96,512]{2,1,0:T(8,128)(2,1)}, bf16[8,96,512]{2,1,0:T(8,128)(2,1)S(1)}, u32[]{:S(2)}) copy-start(bf16[8,96,512]{2,1,0:T(8,128)(2,1)S(1)} %pad_maximum_fusion.2.refs_2_) | copy-start | bytes 2359300
  61.8 22.4 %collective-permute-start.4 = (bf16[8,96,512]{2,1,0:T(8,128)(2,1)S(1)}, bf16[8,96,512]{2,1,0:T(8,128)(2,1)}, u32[]{:S(2)}, u32[]{:S(2)}) collective-permute-start(bf16[8,96,512]{2,1,0:T(8,128)(2,1)S(1)} %pad_maximum_fusion.2.refs_2_), channel_id=1, source_target_pairs={{0,2},{1,3},{2,0},{3,1},{4,6},{5,7},{6,4},{7,5},{8,10},{9,11},{10,... | collective-permute-start | bytes 2359304 | tf_op jit(solution)/shard_map/ppermute | solution.py:575
  65.0 28.0 %copy-start.7 = (bf16[8,128,512]{2,1,0:T(8,128)(2,1)}, bf16[8,128,512]{2,1,0:T(8,128)(2,1)S(1)}, u32[]{:S(2)}) copy-start(bf16[8,128,512]{2,1,0:T(8,128)(2,1)S(1)} %pad_maximum_fusion.1.own_low) | copy-start | bytes 3145732
  65.0 27.9 %collective-permute-start.10 = (bf16[8,128,512]{2,1,0:T(8,128)(2,1)S(1)}, bf16[8,128,512]{2,1,0:T(8,128)(2,1)}, u32[]{:S(2)}, u32[]{:S(2)}) collective-permute-start(bf16[8,128,512]{2,1,0:T(8,128)(2,1)S(1)} %pad_maximum_fusion.1.own_low), channel_id=1, source_target_pairs={{0,2},{1,3},{2,0},{3,1},{4,6},{5,7},{6,4},{7,5},{8,10},{9,11},{10,... | collective-permute-start | bytes 3145736 | tf_op jit(solution)/shard_map/ppermute | solution.py:575
  68.4 4.7 %collective-permute-start.14 = (bf16[1,80,512]{2,1,0:T(8,128)(2,1)S(1)}, bf16[1,80,512]{2,1,0:T(8,128)(2,1)S(1)}, u32[]{:S(2)}, u32[]{:S(2)}) collective-permute-start(bf16[1,80,512]{2,1,0:T(8,128)(2,1)S(1)} %slice_bitcast_fusion.4), channel_id=1, source_target_pairs={{0,4},{1,5},{2,6},{3,7},{4,0},{5,1},{6,2},{7,3},{8,12},{9,13},{10,... | collective-permute-start | bytes 245768 | tf_op jit(solution)/shard_map/ppermute | solution.py:575
  73.1 8.0 %collective-permute-start.15 = (bf16[2,80,512]{2,1,0:T(8,128)(2,1)S(1)}, bf16[2,80,512]{2,1,0:T(8,128)(2,1)S(1)}, u32[]{:S(2)}, u32[]{:S(2)}) collective-permute-start(bf16[2,80,512]{2,1,0:T(8,128)(2,1)S(1)} %pad_maximum_fusion.18), channel_id=1, source_target_pairs={{0,8},{1,9},{2,10},{3,11},{4,12},{5,13},{6,14},{7,15},{8,0},{9,1},... | collective-permute-start | bytes 491528 | tf_op jit(solution)/shard_map/ppermute | solution.py:575
  75.5 23.9 %collective-permute-start.5 = (bf16[8,96,512]{2,1,0:T(8,128)(2,1)S(1)}, bf16[8,96,512]{2,1,0:T(8,128)(2,1)}, u32[]{:S(2)}, u32[]{:S(2)}) collective-permute-start(bf16[8,96,512]{2,1,0:T(8,128)(2,1)S(1)} %pad_maximum_fusion.2.refs_2_), channel_id=1, source_target_pairs={{0,16},{16,0},{1,17},{17,1},{2,18},{18,2},{3,19},{19,3},{4,20},{20... | collective-permute-start | bytes 2359304 | tf_op jit(solution)/shard_map/ppermute | solution.py:579
  82.0 11.0 %collective-permute-start.16 = (bf16[4,80,512]{2,1,0:T(8,128)(2,1)}, bf16[4,80,512]{2,1,0:T(8,128)(2,1)}, u32[]{:S(2)}, u32[]{:S(2)}) collective-permute-start(bf16[4,80,512]{2,1,0:T(8,128)(2,1)} %pad_maximum_fusion.14), channel_id=1, source_target_pairs={{0,1},{1,0},{2,3},{3,2},{4,5},{5,4},{6,7},{7,6},{8,9},{9,8},{10,11... | collective-permute-start | bytes 983048 | tf_op jit(solution)/shard_map/ppermute | solution.py:575
  83.7 39.7 %copy-start.6 = (bf16[8,160,512]{2,1,0:T(8,128)(2,1)}, bf16[8,160,512]{2,1,0:T(8,128)(2,1)S(1)}, u32[]{:S(2)}) copy-start(bf16[8,160,512]{2,1,0:T(8,128)(2,1)S(1)} %pad_maximum_fusion.own_low) | copy-start | bytes 3932164
  83.7 40.4 %collective-permute-start.23 = (bf16[8,160,512]{2,1,0:T(8,128)(2,1)S(1)}, bf16[8,160,512]{2,1,0:T(8,128)(2,1)}, u32[]{:S(2)}, u32[]{:S(2)}) collective-permute-start(bf16[8,160,512]{2,1,0:T(8,128)(2,1)S(1)} %pad_maximum_fusion.own_low), channel_id=1, source_target_pairs={{0,2},{1,3},{2,0},{3,1},{4,6},{5,7},{6,4},{7,5},{8,10},{9,11},{10,... | collective-permute-start | bytes 3932168 | tf_op jit(solution)/shard_map/ppermute | solution.py:575
  84.2 18.8 %collective-permute-start.6 = (bf16[8,96,512]{2,1,0:T(8,128)(2,1)}, bf16[8,96,512]{2,1,0:T(8,128)(2,1)}, u32[]{:S(2)}, u32[]{:S(2)}) collective-permute-start(bf16[8,96,512]{2,1,0:T(8,128)(2,1)} %collective-permute-done.4.refs_3_), channel_id=1, source_target_pairs={{0,16},{16,0},{1,17},{17,1},{2,18},{18,2},{3,19},{19,3},{4,20},{20... | collective-permute-start | bytes 2359304 | tf_op jit(solution)/shard_map/ppermute | solution.py:579
  92.9 31.1 %collective-permute-start.11 = (bf16[8,128,512]{2,1,0:T(8,128)(2,1)S(1)}, bf16[8,128,512]{2,1,0:T(8,128)(2,1)S(1)}, u32[]{:S(2)}, u32[]{:S(2)}) collective-permute-start(bf16[8,128,512]{2,1,0:T(8,128)(2,1)S(1)} %pad_maximum_fusion.1.own_low), channel_id=1, source_target_pairs={{0,16},{16,0},{1,17},{17,1},{2,18},{18,2},{3,19},{19,3},{4,20},{20... | collective-permute-start | bytes 3145736 | tf_op jit(solution)/shard_map/ppermute | solution.py:579
  92.9 31.6 %collective-permute-start.12 = (bf16[8,128,512]{2,1,0:T(8,128)(2,1)}, bf16[8,128,512]{2,1,0:T(8,128)(2,1)S(1)}, u32[]{:S(2)}, u32[]{:S(2)}) collective-permute-start(bf16[8,128,512]{2,1,0:T(8,128)(2,1)} %collective-permute-done.10.own_high), channel_id=1, source_target_pairs={{0,16},{16,0},{1,17},{17,1},{2,18},{18,2},{3,19},{19,3},{4,20},{20... | collective-permute-start | bytes 3145736 | tf_op jit(solution)/shard_map/ppermute | solution.py:579
  99.4 24.0 %collective-permute-start.17 = (bf16[8,80,512]{2,1,0:T(8,128)(2,1)}, bf16[8,80,512]{2,1,0:T(8,128)(2,1)}, u32[]{:S(2)}, u32[]{:S(2)}) collective-permute-start(bf16[8,80,512]{2,1,0:T(8,128)(2,1)} %pad_maximum_fusion.8.refs_4_), channel_id=1, source_target_pairs={{0,2},{1,3},{2,0},{3,1},{4,6},{5,7},{6,4},{7,5},{8,10},{9,11},{10,... | collective-permute-start | bytes 1966088 | tf_op jit(solution)/shard_map/ppermute | solution.py:575
  103.0 37.3 %collective-permute-start.18 = (bf16[8,80,512]{2,1,0:T(8,128)(2,1)}, bf16[8,80,512]{2,1,0:T(8,128)(2,1)}, u32[]{:S(2)}, u32[]{:S(2)}) collective-permute-start(bf16[8,80,512]{2,1,0:T(8,128)(2,1)} %pad_maximum_fusion.8.refs_4_), channel_id=1, source_target_pairs={{0,16},{16,0},{1,17},{17,1},{2,18},{18,2},{3,19},{19,3},{4,20},{20... | collective-permute-start | bytes 1966088 | tf_op jit(solution)/shard_map/ppermute | solution.py:579
  123.4 37.3 %collective-permute-start.24 = (bf16[8,160,512]{2,1,0:T(8,128)(2,1)S(1)}, bf16[8,160,512]{2,1,0:T(8,128)(2,1)}, u32[]{:S(2)}, u32[]{:S(2)}) collective-permute-start(bf16[8,160,512]{2,1,0:T(8,128)(2,1)S(1)} %pad_maximum_fusion.own_low), channel_id=1, source_target_pairs={{0,16},{16,0},{1,17},{17,1},{2,18},{18,2},{3,19},{19,3},{4,20},{20... | collective-permute-start | bytes 3932168 | tf_op jit(solution)/shard_map/ppermute | solution.py:579
  124.0 16.3 %collective-permute-start.19 = (bf16[8,80,512]{2,1,0:T(8,128)(2,1)}, bf16[8,80,512]{2,1,0:T(8,128)(2,1)}, u32[]{:S(2)}, u32[]{:S(2)}) collective-permute-start(bf16[8,80,512]{2,1,0:T(8,128)(2,1)} %collective-permute-done.17.refs_5_), channel_id=1, source_target_pairs={{0,16},{16,0},{1,17},{17,1},{2,18},{18,2},{3,19},{19,3},{4,20},{20... | collective-permute-start | bytes 1966088 | tf_op jit(solution)/shard_map/ppermute | solution.py:579
  124.1 36.7 %collective-permute-start.25 = (bf16[8,160,512]{2,1,0:T(8,128)(2,1)}, bf16[8,160,512]{2,1,0:T(8,128)(2,1)S(1)}, u32[]{:S(2)}, u32[]{:S(2)}) collective-permute-start(bf16[8,160,512]{2,1,0:T(8,128)(2,1)} %collective-permute-done.23.own_high), channel_id=1, source_target_pairs={{0,16},{16,0},{1,17},{17,1},{2,18},{18,2},{3,19},{19,3},{4,20},{20... | collective-permute-start | bytes 3932168 | tf_op jit(solution)/shard_map/ppermute | solution.py:579
  136.6 3.7 collective-permute-start.13
  180.0 49.7 %collective-permute-start.46 = (bf16[16,32,512]{2,1,0:T(8,128)(2,1)}, bf16[16,32,512]{2,1,0:T(8,128)(2,1)S(1)}, u32[]{:S(2)}, u32[]{:S(2)}) collective-permute-start(bf16[16,32,512]{2,1,0:T(8,128)(2,1)} %get-tuple-element.135), channel_id=1, source_target_pairs={{0,16},{16,0},{1,17},{17,1},{2,18},{18,2},{3,19},{19,3},{4,20},{20... | collective-permute-start | bytes 1572872 | tf_op jit(solution)/shard_map/ppermute | solution.py:579
  217.8 45.7 %collective-permute-start.36 = (bf16[16,80,512]{2,1,0:T(8,128)(2,1)}, bf16[16,80,512]{2,1,0:T(8,128)(2,1)S(1)}, u32[]{:S(2)}, u32[]{:S(2)}) collective-permute-start(bf16[16,80,512]{2,1,0:T(8,128)(2,1)} %get-tuple-element.131), channel_id=1, source_target_pairs={{0,16},{16,0},{1,17},{17,1},{2,18},{18,2},{3,19},{19,3},{4,20},{20... | collective-permute-start | bytes 3932168 | tf_op jit(solution)/shard_map/ppermute | solution.py:579
  230.0 28.2 %collective-permute-start.47 = (bf16[8,32,512]{2,1,0:T(8,128)(2,1)S(1)}, bf16[8,32,512]{2,1,0:T(8,128)(2,1)S(1)}, u32[]{:S(2)}, u32[]{:S(2)}) collective-permute-start(bf16[8,32,512]{2,1,0:T(8,128)(2,1)S(1)} %slice.839), channel_id=1, source_target_pairs={{0,2},{1,3},{2,0},{3,1},{4,6},{5,7},{6,4},{7,5},{8,10},{9,11},{10,... | collective-permute-start | bytes 786440 | tf_op jit(solution)/shard_map/ppermute | solution.py:575
  231.2 26.8 %copy-start.41 = (bf16[16,128,512]{2,1,0:T(8,128)(2,1)S(1)}, bf16[16,128,512]{2,1,0:T(8,128)(2,1)}, u32[]{:S(2)}) copy-start(bf16[16,128,512]{2,1,0:T(8,128)(2,1)} %get-tuple-element.129) | copy-start | bytes 6291460
  231.2 28.0 %copy-start.40 = (bf16[16,128,512]{2,1,0:T(8,128)(2,1)S(1)}, bf16[16,128,512]{2,1,0:T(8,128)(2,1)}, u32[]{:S(2)}) copy-start(bf16[16,128,512]{2,1,0:T(8,128)(2,1)} %get-tuple-element.133) | copy-start | bytes 6291460
  257.6 16.6 %collective-permute-start.26 = (bf16[16,96,512]{2,1,0:T(8,128)(2,1)}, bf16[16,96,512]{2,1,0:T(8,128)(2,1)S(1)}, u32[]{:S(2)}, u32[]{:S(2)}) collective-permute-start(bf16[16,96,512]{2,1,0:T(8,128)(2,1)} %get-tuple-element.127), channel_id=1, source_target_pairs={{0,16},{16,0},{1,17},{17,1},{2,18},{18,2},{3,19},{19,3},{4,20},{20... | collective-permute-start | bytes 4718600 | tf_op jit(solution)/shard_map/ppermute | solution.py:579
  258.0 18.6 %collective-permute-start.31 = (bf16[16,128,512]{2,1,0:T(8,128)(2,1)S(1)}, bf16[16,128,512]{2,1,0:T(8,128)(2,1)S(1)}, u32[]{:S(2)}, u32[]{:S(2)}) collective-permute-start(bf16[16,128,512]{2,1,0:T(8,128)(2,1)S(1)} %copy-done.41), channel_id=1, source_target_pairs={{0,16},{16,0},{1,17},{17,1},{2,18},{18,2},{3,19},{19,3},{4,20},{20... | collective-permute-start | bytes 6291464 | tf_op jit(solution)/shard_map/ppermute | solution.py:579
  258.3 5.0 %collective-permute-start.48 = (bf16[4,32,512]{2,1,0:T(8,128)(2,1)S(1)}, bf16[4,32,512]{2,1,0:T(8,128)(2,1)S(1)}, u32[]{:S(2)}, u32[]{:S(2)}) collective-permute-start(bf16[4,32,512]{2,1,0:T(8,128)(2,1)S(1)} %slice.844), channel_id=1, source_target_pairs={{0,1},{1,0},{2,3},{3,2},{4,5},{5,4},{6,7},{7,6},{8,9},{9,8},{10,11... | collective-permute-start | bytes 393224 | tf_op jit(solution)/shard_map/ppermute | solution.py:575
  259.2 30.9 %collective-permute-start.41 = (bf16[16,128,512]{2,1,0:T(8,128)(2,1)S(1)}, bf16[16,128,512]{2,1,0:T(8,128)(2,1)S(1)}, u32[]{:S(2)}, u32[]{:S(2)}) collective-permute-start(bf16[16,128,512]{2,1,0:T(8,128)(2,1)S(1)} %copy-done.40), channel_id=1, source_target_pairs={{0,16},{16,0},{1,17},{17,1},{2,18},{18,2},{3,19},{19,3},{4,20},{20... | collective-permute-start | bytes 6291464 | tf_op jit(solution)/shard_map/ppermute | solution.py:579
  263.3 6.2 %collective-permute-start.49 = (bf16[2,32,512]{2,1,0:T(8,128)(2,1)S(1)}, bf16[2,32,512]{2,1,0:T(8,128)(2,1)S(1)}, u32[]{:S(2)}, u32[]{:S(2)}) collective-permute-start(bf16[2,32,512]{2,1,0:T(8,128)(2,1)S(1)} %slice.849), channel_id=1, source_target_pairs={{0,8},{1,9},{2,10},{3,11},{4,12},{5,13},{6,14},{7,15},{8,0},{9,1},... | collective-permute-start | bytes 196616 | tf_op jit(solution)/shard_map/ppermute | solution.py:575
  264.0 10.9 %collective-permute-start.37 = (bf16[8,80,512]{2,1,0:T(8,128)(2,1)S(1)}, bf16[8,80,512]{2,1,0:T(8,128)(2,1)S(1)}, u32[]{:S(2)}, u32[]{:S(2)}) collective-permute-start(bf16[8,80,512]{2,1,0:T(8,128)(2,1)S(1)} %slice.834), channel_id=1, source_target_pairs={{0,2},{1,3},{2,0},{3,1},{4,6},{5,7},{6,4},{7,5},{8,10},{9,11},{10,... | collective-permute-start | bytes 1966088 | tf_op jit(solution)/shard_map/ppermute | solution.py:575
  269.6 4.0 %collective-permute-start.50 = (bf16[1,32,512]{2,1,0:T(8,128)(2,1)S(1)}, bf16[1,32,512]{2,1,0:T(8,128)(2,1)S(1)}, u32[]{:S(2)}, u32[]{:S(2)}) collective-permute-start(bf16[1,32,512]{2,1,0:T(8,128)(2,1)S(1)} %slice.850), channel_id=1, source_target_pairs={{0,4},{1,5},{2,6},{3,7},{4,0},{5,1},{6,2},{7,3},{8,12},{9,13},{10,... | collective-permute-start | bytes 98312 | tf_op jit(solution)/shard_map/ppermute | solution.py:575
  274.8 13.9 %collective-permute-start.27 = (bf16[8,96,512]{2,1,0:T(8,128)(2,1)S(1)}, bf16[8,96,512]{2,1,0:T(8,128)(2,1)S(1)}, u32[]{:S(2)}, u32[]{:S(2)}) collective-permute-start(bf16[8,96,512]{2,1,0:T(8,128)(2,1)S(1)} %slice.833), channel_id=1, source_target_pairs={{0,2},{1,3},{2,0},{3,1},{4,6},{5,7},{6,4},{7,5},{8,10},{9,11},{10,... | collective-permute-start | bytes 2359304 | tf_op jit(solution)/shard_map/ppermute | solution.py:575
  275.1 10.7 %collective-permute-start.38 = (bf16[4,80,512]{2,1,0:T(8,128)(2,1)S(1)}, bf16[4,80,512]{2,1,0:T(8,128)(2,1)S(1)}, u32[]{:S(2)}, u32[]{:S(2)}) collective-permute-start(bf16[4,80,512]{2,1,0:T(8,128)(2,1)S(1)} %slice.838), channel_id=1, source_target_pairs={{0,1},{1,0},{2,3},{3,2},{4,5},{5,4},{6,7},{7,6},{8,9},{9,8},{10,11... | collective-permute-start | bytes 983048 | tf_op jit(solution)/shard_map/ppermute | solution.py:575
  277.5 33.0 %collective-permute-start.32 = (bf16[8,128,512]{2,1,0:T(8,128)(2,1)S(1)}, bf16[8,128,512]{2,1,0:T(8,128)(2,1)S(1)}, u32[]{:S(2)}, u32[]{:S(2)}) collective-permute-start(bf16[8,128,512]{2,1,0:T(8,128)(2,1)S(1)} %slice.832), channel_id=1, source_target_pairs={{0,2},{1,3},{2,0},{3,1},{4,6},{5,7},{6,4},{7,5},{8,10},{9,11},{10,... | collective-permute-start | bytes 3145736 | tf_op jit(solution)/shard_map/ppermute | solution.py:575
  286.0 8.0 %collective-permute-start.39 = (bf16[2,80,512]{2,1,0:T(8,128)(2,1)S(1)}, bf16[2,80,512]{2,1,0:T(8,128)(2,1)S(1)}, u32[]{:S(2)}, u32[]{:S(2)}) collective-permute-start(bf16[2,80,512]{2,1,0:T(8,128)(2,1)S(1)} %slice.843), channel_id=1, source_target_pairs={{0,8},{1,9},{2,10},{3,11},{4,12},{5,13},{6,14},{7,15},{8,0},{9,1},... | collective-permute-start | bytes 491528 | tf_op jit(solution)/shard_map/ppermute | solution.py:575
  289.1 12.1 %collective-permute-start.28 = (bf16[4,96,512]{2,1,0:T(8,128)(2,1)S(1)}, bf16[4,96,512]{2,1,0:T(8,128)(2,1)S(1)}, u32[]{:S(2)}, u32[]{:S(2)}) collective-permute-start(bf16[4,96,512]{2,1,0:T(8,128)(2,1)S(1)} %slice.837), channel_id=1, source_target_pairs={{0,1},{1,0},{2,3},{3,2},{4,5},{5,4},{6,7},{7,6},{8,9},{9,8},{10,11... | collective-permute-start | bytes 1179656 | tf_op jit(solution)/shard_map/ppermute | solution.py:575
  290.9 29.5 %collective-permute-start.42 = (bf16[8,128,512]{2,1,0:T(8,128)(2,1)S(1)}, bf16[8,128,512]{2,1,0:T(8,128)(2,1)S(1)}, u32[]{:S(2)}, u32[]{:S(2)}) collective-permute-start(bf16[8,128,512]{2,1,0:T(8,128)(2,1)S(1)} %slice.831), channel_id=1, source_target_pairs={{0,2},{1,3},{2,0},{3,1},{4,6},{5,7},{6,4},{7,5},{8,10},{9,11},{10,... | collective-permute-start | bytes 3145736 | tf_op jit(solution)/shard_map/ppermute | solution.py:575
  294.0 9.4 %collective-permute-start.40 = (bf16[1,80,512]{2,1,0:T(8,128)(2,1)S(1)}, bf16[1,80,512]{2,1,0:T(8,128)(2,1)S(1)}, u32[]{:S(2)}, u32[]{:S(2)}) collective-permute-start(bf16[1,80,512]{2,1,0:T(8,128)(2,1)S(1)} %slice.848), channel_id=1, source_target_pairs={{0,4},{1,5},{2,6},{3,7},{4,0},{5,1},{6,2},{7,3},{8,12},{9,13},{10,... | collective-permute-start | bytes 245768 | tf_op jit(solution)/shard_map/ppermute | solution.py:575
  301.3 8.7 %collective-permute-start.29 = (bf16[2,96,512]{2,1,0:T(8,128)(2,1)S(1)}, bf16[2,96,512]{2,1,0:T(8,128)(2,1)S(1)}, u32[]{:S(2)}, u32[]{:S(2)}) collective-permute-start(bf16[2,96,512]{2,1,0:T(8,128)(2,1)S(1)} %slice.842), channel_id=1, source_target_pairs={{0,8},{1,9},{2,10},{3,11},{4,12},{5,13},{6,14},{7,15},{8,0},{9,1},... | collective-permute-start | bytes 589832 | tf_op jit(solution)/shard_map/ppermute | solution.py:575
  310.1 11.7 %collective-permute-start.30 = (bf16[1,96,512]{2,1,0:T(8,128)(2,1)S(1)}, bf16[1,96,512]{2,1,0:T(8,128)(2,1)S(1)}, u32[]{:S(2)}, u32[]{:S(2)}) collective-permute-start(bf16[1,96,512]{2,1,0:T(8,128)(2,1)S(1)} %slice.847), channel_id=1, source_target_pairs={{0,4},{1,5},{2,6},{3,7},{4,0},{5,1},{6,2},{7,3},{8,12},{9,13},{10,... | collective-permute-start | bytes 294920 | tf_op jit(solution)/shard_map/ppermute | solution.py:575
  310.9 11.7 %collective-permute-start.33 = (bf16[4,128,512]{2,1,0:T(8,128)(2,1)S(1)}, bf16[4,128,512]{2,1,0:T(8,128)(2,1)S(1)}, u32[]{:S(2)}, u32[]{:S(2)}) collective-permute-start(bf16[4,128,512]{2,1,0:T(8,128)(2,1)S(1)} %slice.836), channel_id=1, source_target_pairs={{0,1},{1,0},{2,3},{3,2},{4,5},{5,4},{6,7},{7,6},{8,9},{9,8},{10,11... | collective-permute-start | bytes 1572872 | tf_op jit(solution)/shard_map/ppermute | solution.py:575
  320.8 9.2 %collective-permute-start.43 = (bf16[4,128,512]{2,1,0:T(8,128)(2,1)S(1)}, bf16[4,128,512]{2,1,0:T(8,128)(2,1)S(1)}, u32[]{:S(2)}, u32[]{:S(2)}) collective-permute-start(bf16[4,128,512]{2,1,0:T(8,128)(2,1)S(1)} %slice.835), channel_id=1, source_target_pairs={{0,1},{1,0},{2,3},{3,2},{4,5},{5,4},{6,7},{7,6},{8,9},{9,8},{10,11... | collective-permute-start | bytes 1572872 | tf_op jit(solution)/shard_map/ppermute | solution.py:575
  322.7 19.3 %collective-permute-start.34 = (bf16[2,128,512]{2,1,0:T(8,128)(2,1)S(1)}, bf16[2,128,512]{2,1,0:T(8,128)(2,1)S(1)}, u32[]{:S(2)}, u32[]{:S(2)}) collective-permute-start(bf16[2,128,512]{2,1,0:T(8,128)(2,1)S(1)} %slice.841), channel_id=1, source_target_pairs={{0,8},{1,9},{2,10},{3,11},{4,12},{5,13},{6,14},{7,15},{8,0},{9,1},... | collective-permute-start | bytes 786440 | tf_op jit(solution)/shard_map/ppermute | solution.py:575
  330.3 16.6 %collective-permute-start.44 = (bf16[2,128,512]{2,1,0:T(8,128)(2,1)S(1)}, bf16[2,128,512]{2,1,0:T(8,128)(2,1)S(1)}, u32[]{:S(2)}, u32[]{:S(2)}) collective-permute-start(bf16[2,128,512]{2,1,0:T(8,128)(2,1)S(1)} %slice.840), channel_id=1, source_target_pairs={{0,8},{1,9},{2,10},{3,11},{4,12},{5,13},{6,14},{7,15},{8,0},{9,1},... | collective-permute-start | bytes 786440 | tf_op jit(solution)/shard_map/ppermute | solution.py:575
  342.2 7.5 %collective-permute-start.35 = (bf16[1,128,512]{2,1,0:T(8,128)(2,1)S(1)}, bf16[1,128,512]{2,1,0:T(8,128)(2,1)S(1)}, u32[]{:S(2)}, u32[]{:S(2)}) collective-permute-start(bf16[1,128,512]{2,1,0:T(8,128)(2,1)S(1)} %slice.846), channel_id=1, source_target_pairs={{0,4},{1,5},{2,6},{3,7},{4,0},{5,1},{6,2},{7,3},{8,12},{9,13},{10,... | collective-permute-start | bytes 393224 | tf_op jit(solution)/shard_map/ppermute | solution.py:575
  347.0 5.4 %collective-permute-start.45 = (bf16[1,128,512]{2,1,0:T(8,128)(2,1)S(1)}, bf16[1,128,512]{2,1,0:T(8,128)(2,1)S(1)}, u32[]{:S(2)}, u32[]{:S(2)}) collective-permute-start(bf16[1,128,512]{2,1,0:T(8,128)(2,1)S(1)} %slice.845), channel_id=1, source_target_pairs={{0,4},{1,5},{2,6},{3,7},{4,0},{5,1},{6,2},{7,3},{8,12},{9,13},{10,... | collective-permute-start | bytes 393224 | tf_op jit(solution)/shard_map/ppermute | solution.py:575
  355.1 1.1 collective-permute-start.52
  355.2 18.8 %collective-permute-start.51 = (f32[256,512]{1,0:T(8,128)S(1)}, f32[256,512]{1,0:T(8,128)S(1)}, u32[]{:S(2)}, u32[]{:S(2)}) collective-permute-start(f32[256,512]{1,0:T(8,128)S(1)} %pad_maximum_fusion.4), channel_id=1, source_target_pairs={{0,16},{16,0},{1,17},{17,1},{2,18},{18,2},{3,19},{19,3},{4,20},{20... | collective-permute-start | bytes 1572872 | tf_op jit(solution)/shard_map/ppermute | solution.py:579
  356.9 3.5 collective-permute-start.53
  361.2 4.4 %collective-permute-start.54 = (f32[1,2]{1,0:T(1,128)S(1)}, f32[1,2]{1,0:T(1,128)S(1)}, u32[]{:S(2)}, u32[]{:S(2)}) collective-permute-start(f32[1,2]{1,0:T(1,128)S(1)} %fusion.45), channel_id=1, source_target_pairs={{0,8},{1,9},{2,10},{3,11},{4,12},{5,13},{6,14},{7,15},{8,0},{9,1},... | collective-permute-start | bytes 32 | tf_op jit(solution)/shard_map/ppermute | solution.py:575
  365.6 3.5 collective-permute-start.55
  369.2 3.5 collective-permute-start.56
  (38 other events, 122.4 us)
